TPU v7x, 128 devices: a whole 4x4x4 slice. The times are simulated.
128 devices in a mesh: chan: 32 (over z, y, core), win: 4 (over x).
Axes of the slice: x: 4, y: 4, z: 4, core: 2. Of those that a mesh axis runs over, the one named last changes fastest.
Arguments:
- spectra: float32 [8, 2, 512, 4096], P('win', None, 'chan'), may hold values from -500 to 500, as said below
- plan: int32 [4], replicated, may hold values from 0 to 31, as said below
- pair_bins: int32 [512, 64, 1], P('chan'), may hold values from 0 to 255; in each aligned block of 1024 rows (0 to 1023, 1024 to 2047, ..., all dimensions but the last counted through in order) at most 8 rows name the same one
Outputs:
- stack: float32 [256, 512], P('chan')
Inputs may be any that keep to these rules, and one draw needn't show every extreme that they name: Float spectra with channel and bin scales of order one to ten. `plan`: 4 distinct block indices. `pair_bins`: among the pairs of one device's receivers (16 channels, aligned blocks of rows), no bin is named more than 8 times, a bound that some block reaches. Every bin is named by some pair.
All inputs are finite; a program needn't handle non-finite values.
Results may differ from a plain program's by a relative error of at most 0.0051.
Values may be sent and summed in bfloat16 or wider, within the bound.
No kernel may reach another device: no remote copies, remote signals or barrier semaphores. Data moves between devices by JAX's collectives and lax.ppermute only.
A program may use at most 64 MiB of HBM per device.

v0:
```python
import math

import jax
import jax.numpy as jnp
from jax import lax
from jax.sharding import PartitionSpec as P

LAGS = 512
BAND = 128
FBLOCK = 512
STEPS = 4
NBINS = 256
CAP = 8


def from_root(value, axis, source):
    kept = jnp.where(lax.axis_index(axis) == source, value, 0).astype(value.dtype)
    return lax.psum(kept, axis)


def whiten(spectra):
    energy = spectra[:, 0] ** 2 + spectra[:, 1] ** 2
    banded = energy.reshape(energy.shape[0], energy.shape[1], -1, BAND)
    band_level = jnp.sqrt(jnp.mean(banded, axis=3) + 1e-06)
    level_full = jnp.repeat(band_level, BAND, axis=2)
    return (spectra / level_full[:, None]).astype(jnp.bfloat16)


def lag_table(offset, span_bins, lag_count, bin_total):
    numbers = offset + 1 + lax.iota(jnp.int32, span_bins)
    shifts = lax.iota(jnp.int32, lag_count) - lag_count // 2
    phase = jnp.mod(numbers[:, None] * shifts[None, :], 2 * bin_total)
    angle = phase.astype(jnp.float32) * (math.pi / bin_total)
    factor = 1.0 / math.sqrt(bin_total)
    return (jnp.stack([jnp.cos(angle), -jnp.sin(angle)]) * factor).astype(jnp.bfloat16)


def cross_rows(source, receiver):
    source_real = jnp.transpose(source[:, 0].astype(jnp.float32), (1, 0, 2))[None]
    source_imaginary = jnp.transpose(source[:, 1].astype(jnp.float32), (1, 0, 2))[None]
    receiver_real = jnp.transpose(receiver[:, 0].astype(jnp.float32), (1, 0, 2))[:, None]
    receiver_imaginary = jnp.transpose(receiver[:, 1].astype(jnp.float32), (1, 0, 2))[:, None]
    product_real = source_real * receiver_real + source_imaginary * receiver_imaginary
    product_imaginary = source_imaginary * receiver_real - source_real * receiver_imaginary
    joined = jnp.stack([product_real, product_imaginary], axis=3).astype(jnp.bfloat16)
    return joined.reshape(joined.shape[0] * joined.shape[1], -1)


def per_device(spectra, plan, pair_bins):
    whitened = whiten(spectra)
    window_count = spectra.shape[0]
    receivers = spectra.shape[2]
    bin_total = spectra.shape[3]
    sources = []
    for source_step in range(STEPS):
        sources.append(from_root(whitened, "chan", plan[source_step]))

    def add_block(block_index, totals):
        block_start = block_index * FBLOCK
        table_block = lag_table(block_start, FBLOCK, LAGS, bin_total)
        table_tiled = jnp.broadcast_to(
            table_block[None], (window_count,) + table_block.shape
        ).reshape(window_count * 2 * FBLOCK, LAGS)
        receiver = lax.dynamic_slice_in_dim(whitened, block_start, FBLOCK, 3)
        updated = []
        for source_step in range(STEPS):
            source = lax.dynamic_slice_in_dim(sources[source_step], block_start, FBLOCK, 3)
            updated.append(
                totals[source_step]
                + jnp.dot(
                    cross_rows(source, receiver), table_tiled, preferred_element_type=jnp.float32
                )
            )
        return tuple(updated)

    initial = tuple(
        (jnp.zeros((receivers * receivers, LAGS), jnp.float32) for source_step in range(STEPS))
    )
    totals = lax.fori_loop(0, bin_total // FBLOCK, add_block, initial)
    traces = jnp.stack(
        [entry.reshape(receivers, receivers, LAGS) for entry in totals], axis=1
    ).reshape(-1, LAGS)
    segment_ids = pair_bins.reshape(-1)
    owners = lax.axis_size("chan")
    pair_total = segment_ids.shape[0]
    ordering = lax.iota(jnp.int32, pair_total)
    earlier = (segment_ids[:, None] == segment_ids[None, :]) & (
        ordering[None, :] < ordering[:, None]
    )
    slot_rank = jnp.sum(earlier.astype(jnp.int32), axis=1)
    slot_index = segment_ids * CAP + slot_rank
    outgoing = jnp.zeros((NBINS * CAP, LAGS), jnp.float32).at[slot_index].set(traces)
    occupied = jnp.zeros((NBINS * CAP,), jnp.float32).at[slot_index].set(1.0)
    outgoing = outgoing.reshape(owners, NBINS // owners, CAP, LAGS)
    occupied = occupied.reshape(owners, NBINS // owners, CAP)
    partial_sums = jnp.sum(
        lax.all_to_all(outgoing, "chan", split_axis=0, concat_axis=0, tiled=True), axis=(0, 2)
    )
    counts = jnp.sum(
        lax.all_to_all(occupied, "chan", split_axis=0, concat_axis=0, tiled=True), axis=(0, 2)
    )
    window_sums = lax.psum(partial_sums, "win")
    window_total = window_count * lax.axis_size("win")
    return window_sums / jnp.sqrt(counts * window_total)[:, None]


def solution(mesh):
    placed = (P("win", None, "chan", None), P(), P("chan", None, None))
    return jax.shard_map(
        per_device, mesh=mesh, in_specs=placed, out_specs=P("chan", None), check_vma=False
    )
```

profile of v0, /device:TPU:0, one launch (start us, length us, event | category | flops | bytes accessed | tf_op | source)
XLA Modules:
  0.0 622.1 jit_solution(17076086751071402284)
XLA Ops:
  17.9 4.3 scatter_custom_fusion.1
  23.0 8.4 %all-to-all-start.1 = ((f32[32,8,8]{2,1,0:T(8,128)}), f32[32,8,8]{2,1,0:T(8,128)S(1)}, u32[]{:S(2)}, u32[]{:S(2)}) async-start(f32[32,8,8]{2,1,0:T(8,128)} %reshape.503), calls=%async_computation.1 | async-start | bytes 262144 | tf_op jit(solution)/shard_map/all_to_all | solution.py:100
  31.5 95.5 %all-reduce.3.cloned.1.call-done = (bf16[2,2,16,4096]{3,2,1,0:T(8,128)(2,1)}, bf16[2,2,16,4096]{3,2,1,0:T(8,128)(2,1)}, bf16[2,2,16,4096]{3,2,1,0:T(8,128)(2,1)}, bf16[2,2,16,4096]{3,2,1,0:T(8,128)(2,1)}) async-done(((bf16[2,2,16,4096]{3,2,1,0:T(8,128)(2,1)}, bf16[2,2,16,4096]{3,2,1,0:T(8,128)(2,1)}, bf16[2,2,16,4096]{3,2,1,0:T(8,128)(2,1)}, bf16[2,2,16,4096]{3,2,1,0:T(8,128)(2,1)}), ...) | async-done | bytes 2097168 | tf_op jit(solution)/shard_map/psum | solution.py:18
  126.9 400.5 %while.22 = (s32[]{:T(128)}, f32[256,512]{1,0:T(8,128)}, f32[256,512]{1,0:T(8,128)}, f32[256,512]{1,0:T(8,128)}, f32[256,512]{1,0:T(8,128)}, /*index=5*/bf16[2,2...) while((s32[]{:T(128)}, f32[256,512]{1,0:T(8,128)}, ...), condition=%wide.region_7.8_spmd.clone, body=%wide.region_6.7_spmd.clone.sunk | while | flops 2170979328 | bytes 59580804 | solution.py:79
  130.0 10.1 %add_convert_fusion.5 = (bf16[16,16,2,1,512]{4,3,2,1,0:T(2,128)(2,1)S(1)}, bf16[16,16,2,1,512]{4,3,2,1,0:T(2,128)(2,1)S(1)}, bf16[16,16,2,1,512]{4,3,2,1,0:T(2,1...) fusion(f32[16,2,512]{2,1,0:T(2,128)S(1)} %copy.45, ...), kind=kLoop, calls=%fused_computation.21.clone.1 | loop fusion | flops 8388608 | bytes 4849664 | tf_op jit(solution)/shard_map/convert.20
  144.1 4.2 fusion.38
  178.8 10.1 %add_convert_fusion.5 = (bf16[16,16,2,1,512]{4,3,2,1,0:T(2,128)(2,1)S(1)}, bf16[16,16,2,1,512]{4,3,2,1,0:T(2,128)(2,1)S(1)}, bf16[16,16,2,1,512]{4,3,2,1,0:T(2,1...) fusion(f32[16,2,512]{2,1,0:T(2,128)S(1)} %copy.45, ...), kind=kLoop, calls=%fused_computation.21.clone.1 | loop fusion | flops 8388608 | bytes 4849664 | tf_op jit(solution)/shard_map/convert.20
  193.0 4.2 fusion.38
  229.1 10.1 %add_convert_fusion.5 = (bf16[16,16,2,1,512]{4,3,2,1,0:T(2,128)(2,1)S(1)}, bf16[16,16,2,1,512]{4,3,2,1,0:T(2,128)(2,1)S(1)}, bf16[16,16,2,1,512]{4,3,2,1,0:T(2,1...) fusion(f32[16,2,512]{2,1,0:T(2,128)S(1)} %copy.45, ...), kind=kLoop, calls=%fused_computation.21.clone.1 | loop fusion | flops 8388608 | bytes 4849664 | tf_op jit(solution)/shard_map/convert.20
  243.2 4.2 fusion.38
  279.3 10.1 %add_convert_fusion.5 = (bf16[16,16,2,1,512]{4,3,2,1,0:T(2,128)(2,1)S(1)}, bf16[16,16,2,1,512]{4,3,2,1,0:T(2,128)(2,1)S(1)}, bf16[16,16,2,1,512]{4,3,2,1,0:T(2,1...) fusion(f32[16,2,512]{2,1,0:T(2,128)S(1)} %copy.45, ...), kind=kLoop, calls=%fused_computation.21.clone.1 | loop fusion | flops 8388608 | bytes 4849664 | tf_op jit(solution)/shard_map/convert.20
  293.5 4.2 fusion.38
  329.6 10.1 %add_convert_fusion.5 = (bf16[16,16,2,1,512]{4,3,2,1,0:T(2,128)(2,1)S(1)}, bf16[16,16,2,1,512]{4,3,2,1,0:T(2,128)(2,1)S(1)}, bf16[16,16,2,1,512]{4,3,2,1,0:T(2,1...) fusion(f32[16,2,512]{2,1,0:T(2,128)S(1)} %copy.45, ...), kind=kLoop, calls=%fused_computation.21.clone.1 | loop fusion | flops 8388608 | bytes 4849664 | tf_op jit(solution)/shard_map/convert.20
  343.7 4.2 fusion.38
  379.8 10.1 %add_convert_fusion.5 = (bf16[16,16,2,1,512]{4,3,2,1,0:T(2,128)(2,1)S(1)}, bf16[16,16,2,1,512]{4,3,2,1,0:T(2,128)(2,1)S(1)}, bf16[16,16,2,1,512]{4,3,2,1,0:T(2,1...) fusion(f32[16,2,512]{2,1,0:T(2,128)S(1)} %copy.45, ...), kind=kLoop, calls=%fused_computation.21.clone.1 | loop fusion | flops 8388608 | bytes 4849664 | tf_op jit(solution)/shard_map/convert.20
  393.9 4.2 fusion.38
  430.1 10.1 %add_convert_fusion.5 = (bf16[16,16,2,1,512]{4,3,2,1,0:T(2,128)(2,1)S(1)}, bf16[16,16,2,1,512]{4,3,2,1,0:T(2,128)(2,1)S(1)}, bf16[16,16,2,1,512]{4,3,2,1,0:T(2,1...) fusion(f32[16,2,512]{2,1,0:T(2,128)S(1)} %copy.45, ...), kind=kLoop, calls=%fused_computation.21.clone.1 | loop fusion | flops 8388608 | bytes 4849664 | tf_op jit(solution)/shard_map/convert.20
  444.2 4.2 fusion.38
  480.3 10.1 %add_convert_fusion.5 = (bf16[16,16,2,1,512]{4,3,2,1,0:T(2,128)(2,1)S(1)}, bf16[16,16,2,1,512]{4,3,2,1,0:T(2,128)(2,1)S(1)}, bf16[16,16,2,1,512]{4,3,2,1,0:T(2,1...) fusion(f32[16,2,512]{2,1,0:T(2,128)S(1)} %copy.45, ...), kind=kLoop, calls=%fused_computation.21.clone.1 | loop fusion | flops 8388608 | bytes 4849664 | tf_op jit(solution)/shard_map/convert.20
  494.4 4.2 fusion.38
  529.2 6.9 %scatter_custom_fusion = f32[2048,512]{1,0:T(8,128)} fusion(s32[1024]{0:T(1024)S(1)} %bitcast.144, f32[1024,512]{1,0:T(8,128)S(1)} %bitcast.141, f32[]{:T(128)} %constant.110.clone.1), kind=kCustom, calls=%fused_computation.56 | custom fusion | bytes 4194308 | tf_op jit(solution)/shard_map/scatter | solution.py:92
  536.1 5.6 all-to-all-start
  541.9 53.3 %all-to-all-done = f32[32,8,8,512]{3,2,1,0:T(8,128)} async-done(((f32[32,8,8,512]{3,2,1,0:T(8,128)}), f32[32,8,8,512]{3,2,1,0:T(8,128)}, u32[]{:S(2)}, u32[]{:S(2)}) %all-to-all-start) | async-done | bytes 4194336 | tf_op jit(solution)/shard_map/all_to_all | solution.py:97
  597.8 16.8 %psum.39 = f32[8,512]{1,0:T(8,128)S(1)} all-reduce(f32[8,512]{1,0:T(8,128)S(1)} %reduce_sum.41), channel_id=1, replica_groups=mesh['chan'=32,'win'=4] {'win'}, use_global_device_ids=true, to_apply=%region_10.11 | all-reduce | flops 4096 | bytes 32768 | tf_op jit(solution)/shard_map/psum | solution.py:102
  (337 shorter events, 300.0 us)
Async XLA Ops:
  6.5 120.4 %all-reduce.3.cloned.1.call-start = ((), (), s32[]{:S(2)}) async-start(), calls=%async_computation.2 | async-start | bytes 4194304 | tf_op jit(solution)/shard_map/psum | solution.py:18
  8.0 4.5 copy-start.5
  23.0 513.1 %all-to-all-start.1 = ((f32[32,8,8]{2,1,0:T(8,128)}), f32[32,8,8]{2,1,0:T(8,128)S(1)}, u32[]{:S(2)}, u32[]{:S(2)}) async-start(f32[32,8,8]{2,1,0:T(8,128)} %reshape.503), calls=%async_computation.1 | async-start | bytes 262144 | tf_op jit(solution)/shard_map/all_to_all | solution.py:100
  197.6 3.1 copy-start.3
  197.6 3.1 copy-start.4
  206.5 3.0 copy-start.2
  247.9 3.1 copy-start.3
  247.9 3.1 copy-start.4
  298.1 3.1 copy-start.3
  298.1 3.1 copy-start.4
  307.0 3.0 copy-start.2
  348.4 3.1 copy-start.3
  348.4 3.1 copy-start.4
  398.6 3.1 copy-start.3
  398.6 3.1 copy-start.4
  407.5 3.0 copy-start.1
  407.5 3.0 copy-start.2
  448.9 3.1 copy-start.3
  448.9 3.1 copy-start.4
  457.8 3.0 copy-start.2
  499.1 3.1 copy-start.3
  499.1 3.1 copy-start.4
  508.0 3.0 copy-start.2
  536.1 59.1 %all-to-all-start = ((f32[32,8,8,512]{3,2,1,0:T(8,128)}), f32[32,8,8,512]{3,2,1,0:T(8,128)}, u32[]{:S(2)}, u32[]{:S(2)}) async-start(f32[32,8,8,512]{3,2,1,0:T(8,128)} %bitcast.139), calls=%async_computation | async-start | bytes 8388608 | tf_op jit(solution)/shard_map/all_to_all | solution.py:97
  (21 other events, 62.0 us)
Sparse Core Ops, SparseCore 0:
  16.1 110.7 all-reduce.2
where the time goes:
time: 625 us; the launch traced here: 622 us
  other arithmetic  244 us (39%)
  waiting for transfers between devices  149 us (24%)
  matrix products  91.5 us (15%)
  local copies, waits for them, and re-layouts  89.9 us (14%)
  blocking collectives  16.8 us (3%)
  between operations  16.1 us (3%)
  starting transfers between devices  14 us (2%)
    another operation x32, other arithmetic, cross_rows(): jnp.stack([product_real, product_imaginary], axis=3).astype(jnp.bfloat16)  96.4 us
    psum x1, waiting for transfers between devices, from_root(): return lax.psum(kept, axis)  95.5 us
    dot_general x32, matrix products, add_block(): jnp.dot(cross_rows(source, receiver), table_tiled, preferred_element_type...  91.5 us
    another operation x8, other arithmetic  80.5 us
    convert_element_type x32, local copies, waits for them, and re-layouts, cross_rows(): jnp.stack([product_real, product_imaginary], axis=3).astype(jnp.bfloat16)  69.6 us
    all_to_all x1, waiting for transfers between devices, per_device(): lax.all_to_all(outgoing, 'chan', split_axis=0, concat_axis=0, tiled=True)  53.3 us
    cos x8, other arithmetic, lag_table(): jnp.cos(angle)  33.5 us
    transpose x24, other arithmetic, cross_rows(): jnp.transpose(source[:, 0].astype(jnp.float32), (1, 0, 2))[None]  19.7 us
  transfers between devices with their start and end apart: 3, of which 2 were waited for; matrix products, arithmetic and copies ran while one was open for 67% of the time, Pallas kernels for 0%

commit v1 on v0

v1 whole, which is shorter than its diff:
```python
import functools
import math

import jax
import jax.numpy as jnp
from jax import lax
from jax.experimental import pallas as pl
from jax.experimental.pallas import tpu as pltpu
from jax.sharding import PartitionSpec as P

LAGS = 512
BAND = 128
STEPS = 4
NBINS = 256
CH = 16
SOURCES = STEPS * CH
JBLK = 4


def whiten_kernel(spectra_ref, bins_ref, out_ref):
    chunks = out_ref.shape[0]
    windows = spectra_ref.shape[0]
    bins = bins_ref[...].astype(jnp.float32)
    bins = jnp.concatenate([bins, jnp.zeros_like(bins)], axis=1).astype(jnp.bfloat16)
    for c in range(chunks):
        lanes = pl.ds(c * BAND, BAND)
        for w in range(windows):
            real = spectra_ref[w, 0, :, lanes]
            imaginary = spectra_ref[w, 1, :, lanes]
            energy = real * real + imaginary * imaginary
            level = jnp.sqrt(jnp.mean(energy, axis=1, keepdims=True) + 1e-06)
            out_ref[c, pl.ds(2 * w * CH, CH), :] = (real / level).astype(jnp.bfloat16)
            out_ref[c, pl.ds((2 * w + 1) * CH, CH), :] = (imaginary / level).astype(jnp.bfloat16)
        out_ref[c, pl.ds(2 * windows * CH, CH), :] = bins


def whiten(spectra, bins):
    windows, _, channels, freq = spectra.shape
    owners = freq // BAND
    rows = 2 * windows * CH + CH
    step = 4
    return pl.pallas_call(
        whiten_kernel,
        grid=(owners // step,),
        in_specs=[
            pl.BlockSpec((windows, 2, channels, step * BAND), lambda i: (0, 0, 0, i)),
            pl.BlockSpec(bins.shape, lambda i: (0, 0)),
        ],
        out_specs=pl.BlockSpec((step, rows, BAND), lambda i: (i, 0, 0)),
        out_shape=jax.ShapeDtypeStruct((owners, rows, BAND), jnp.bfloat16),
    )(spectra, bins)


def bin_kernel(windows, plan_ref, x_ref, table_ref, out_ref, rec_ref, src_ref, bt_ref, sums_ref):
    owners = x_ref.shape[0]
    channels = owners * CH
    parts = 2 * windows
    for p in range(parts):
        rec_ref[p] = x_ref[:, pl.ds(p * CH, CH), :].reshape(channels, BAND)
    for q in range(STEPS):
        for p in range(parts):
            slab = x_ref[plan_ref[q], pl.ds(p * CH, CH), :].astype(jnp.float32)
            for j in range(CH):
                row = jnp.broadcast_to(slab[j:j + 1, :], (CH, BAND))
                src_ref[q * CH + j, p] = row.astype(jnp.bfloat16)
    bins = x_ref[:, pl.ds(parts * CH, CH), :].reshape(channels, BAND).astype(jnp.float32)
    turned = bins.T
    for j in range(SOURCES):
        row = jnp.broadcast_to(turned[j:j + 1, :], (CH, channels))
        bt_ref[j] = row.astype(jnp.bfloat16)
    sums_ref[...] = jnp.zeros_like(sums_ref)

    def step(index, carry):
        numbers = lax.broadcasted_iota(jnp.int32, (NBINS, channels), 0).astype(jnp.float32)
        numbers = numbers.astype(jnp.bfloat16)
        one = jnp.ones((), jnp.bfloat16)
        zero = jnp.zeros((), jnp.bfloat16)
        hots = []
        crosses = []
        for k in range(JBLK):
            j = index * JBLK + k
            named = jnp.broadcast_to(bt_ref[j][None], (NBINS // CH, CH, channels))
            hots.append(jnp.where(numbers == named.reshape(NBINS, channels), one, zero))
            total_real = None
            for w in range(windows):
                sr = src_ref[j, 2 * w][None]
                si = src_ref[j, 2 * w + 1][None]
                rr = rec_ref[2 * w].reshape(owners, CH, BAND)
                ri = rec_ref[2 * w + 1].reshape(owners, CH, BAND)
                real = sr * rr + si * ri
                imaginary = si * rr - sr * ri
                if total_real is None:
                    total_real, total_imaginary = real, imaginary
                else:
                    total_real = total_real + real
                    total_imaginary = total_imaginary + imaginary
            crosses.append(
                jnp.concatenate([total_real, total_imaginary], axis=2).reshape(channels, 2 * BAND)
            )
        hot = jnp.concatenate(hots, axis=1)
        cross = jnp.concatenate(crosses, axis=0)
        sums_ref[...] += jnp.dot(hot, cross, preferred_element_type=jnp.float32)
        return carry

    lax.fori_loop(0, SOURCES // JBLK, step, 0)
    sums = sums_ref[...]
    high = sums.astype(jnp.bfloat16)
    low = (sums - high.astype(jnp.float32)).astype(jnp.bfloat16)
    table = table_ref[...]
    lags = jnp.dot(high, table, preferred_element_type=jnp.float32)
    lags = lags + jnp.dot(low, table, preferred_element_type=jnp.float32)
    out_ref[...] = lags.astype(jnp.bfloat16)


def bin_sums(plan, gathered, table, windows):
    owners, rows, _ = gathered.shape
    channels = owners * CH
    vmem = pl.BlockSpec(memory_space=pltpu.VMEM)
    return pl.pallas_call(
        functools.partial(bin_kernel, windows),
        in_specs=[pl.BlockSpec(memory_space=pltpu.SMEM), vmem, vmem],
        out_specs=vmem,
        out_shape=jax.ShapeDtypeStruct((NBINS, LAGS), jnp.bfloat16),
        scratch_shapes=[
            pltpu.VMEM((2 * windows, channels, BAND), jnp.bfloat16),
            pltpu.VMEM((SOURCES, 2 * windows, CH, BAND), jnp.bfloat16),
            pltpu.VMEM((SOURCES, CH, channels), jnp.bfloat16),
            pltpu.VMEM((NBINS, 2 * BAND), jnp.float32),
        ],
        compiler_params=pltpu.CompilerParams(vmem_limit_bytes=40 * 1024 * 1024),
    )(plan, gathered, table)


def lag_table(offset, span_bins, lag_count, bin_total):
    numbers = offset + 1 + lax.iota(jnp.int32, span_bins)
    shifts = lax.iota(jnp.int32, lag_count) - lag_count // 2
    phase = jnp.mod(numbers[:, None] * shifts[None, :], 2 * bin_total)
    angle = phase.astype(jnp.float32) * (math.pi / bin_total)
    factor = 1.0 / math.sqrt(bin_total)
    table = (jnp.stack([jnp.cos(angle), -jnp.sin(angle)]) * factor).astype(jnp.bfloat16)
    return table.reshape(2 * span_bins, lag_count)


def per_device(spectra, plan, pair_bins):
    windows = spectra.shape[0]
    freq = spectra.shape[3]
    owners = lax.axis_size("chan")
    win_size = lax.axis_size("win")
    own = lax.axis_index("chan")
    outgoing = whiten(spectra, pair_bins.reshape(CH, SOURCES))
    gathered = lax.all_to_all(outgoing, "chan", split_axis=0, concat_axis=0, tiled=True)
    table = lag_table(own * BAND, BAND, LAGS, freq)
    partial = bin_sums(plan, gathered, table, windows)
    bin_block = NBINS // owners
    arrived = lax.all_to_all(
        partial.reshape(owners, bin_block, LAGS), "chan", split_axis=0, concat_axis=0, tiled=True
    )
    total = jnp.sum(arrived.astype(jnp.float32), axis=0)
    named = gathered[:, 2 * windows * CH:, :SOURCES].astype(jnp.float32)
    mine = (own * bin_block + lax.iota(jnp.int32, bin_block)).astype(jnp.float32)
    counts = jnp.sum((named[None] == mine[:, None, None, None]).astype(jnp.float32), axis=(1, 2, 3))
    summed = total
    for d in range(1, win_size):
        summed = summed + lax.ppermute(
            total, "win", [(i, (i + d) % win_size) for i in range(win_size)]
        )
    return summed / jnp.sqrt(counts * (windows * win_size))[:, None]


def solution(mesh):
    placed = (P("win", None, "chan", None), P(), P("chan", None, None))
    return jax.shard_map(
        per_device, mesh=mesh, in_specs=placed, out_specs=P("chan", None), check_vma=False
    )
```

time: 625 us -> 63.8 us (0.10)
  other arithmetic: 244 us -> 2.38 us
  waiting for transfers between devices: 149 us -> 24.5 us
  matrix products: 91.5 us -> 0 us
  local copies, waits for them, and re-layouts: 89.9 us -> 0.01 us
  Pallas kernels: 0 us -> 19.6 us
  blocking collectives: 16.8 us -> 0 us
  between operations: 16.1 us -> 0.08 us
    another operation x41 -> x0, other arithmetic: 179 us -> none  [the longest x32 96.4 us: cross_rows(): jnp.stack([product_real, product_imaginary], axis=3).astype(jnp.bfloat16)]
    psum x1 -> x0, waiting for transfers between devices: 95.5 us -> none  [from_root(): return lax.psum(kept, axis)]
    dot_general x32 -> x0, matrix products: 91.5 us -> none  [add_block(): jnp.dot(cross_rows(source, receiver), table_tiled, preferred_element_type...]
    convert_element_type x32 -> x0, local copies, waits for them, and re-layouts: 69.6 us -> none  [cross_rows(): jnp.stack([product_real, product_imaginary], axis=3).astype(jnp.bfloat16)]
    all_to_all x1, waiting for transfers between devices: 53.3 us -> 12 us  [per_device(): lax.all_to_all(outgoing, 'chan', split_axis=0, concat_axis=0, tiled=True)]
    cos x8 -> x1, other arithmetic: 33.5 us -> 1.1 us  [lag_table(): jnp.cos(angle)]
    transpose x24 -> x0, other arithmetic: 19.7 us -> none  [cross_rows(): jnp.transpose(source[:, 0].astype(jnp.float32), (1, 0, 2))[None]]
    pallas_call x0 -> x2, Pallas kernels: none -> 19.6 us  [the longest x1 14.1 us: bin_sums(): pl.pallas_call(functools.partial(bin_kernel, windows), in_specs=[pl.Block...]
  transfers between devices with their start and end apart: 3 -> 5, of which waited for: 2 -> 4; matrix products, arithmetic and copies ran while one was open for 67% -> 3% of each run, Pallas kernels for 0% -> 0%
where the time goes in v1:
time: 63.8 us; the launch traced here: 63.4 us
  waiting for transfers between devices  24.5 us (38%)
  Pallas kernels  19.6 us (31%)
  starting transfers between devices  16.9 us (26%)
  other arithmetic  2.38 us (4%)
    pallas_call x1, Pallas kernels, bin_sums(): pl.pallas_call(functools.partial(bin_kernel, windows), in_specs=[pl.Block...  14.1 us
    all_to_all x1, waiting for transfers between devices, per_device(): lax.all_to_all(outgoing, 'chan', split_axis=0, concat_axis=0, tiled=True)  12 us
    all_to_all x1, starting transfers between devices, per_device(): lax.all_to_all(outgoing, 'chan', split_axis=0, concat_axis=0, tiled=True)  8.55 us
    all_to_all x1, waiting for transfers between devices, per_device(): lax.all_to_all(partial.reshape(owners, bin_block, LAGS), 'chan', split_ax...  8.4 us
    pallas_call x1, Pallas kernels, whiten(): pl.pallas_call(whiten_kernel, grid=(owners // step,), in_specs=[pl.BlockS...  5.49 us
    ppermute x3, starting transfers between devices, per_device(): lax.ppermute(total, 'win', [(i, (i + d) % win_size) for i in range(win_si...  4.51 us
    ppermute x3, waiting for transfers between devices, per_device(): lax.ppermute(total, 'win', [(i, (i + d) % win_size) for i in range(win_si...  4.05 us
    all_to_all x1, starting transfers between devices, per_device(): lax.all_to_all(partial.reshape(owners, bin_block, LAGS), 'chan', split_ax...  3.87 us
  transfers between devices with their start and end apart: 5, of which 4 were waited for; matrix products, arithmetic and copies ran while one was open for 3% of the time, Pallas kernels for 0%

profile of v1, /device:TPU:0, one launch (start us, length us, event | category | flops | bytes accessed | tf_op | source)
XLA Modules:
  0.0 63.4 jit_solution(11582287698945633538)
XLA Ops:
  0.0 5.5 %shard_map.37 = bf16[32,80,128]{2,1,0:T(8,128)(2,1)} custom-call(f32[2,2,16,4096]{3,2,1,0:T(8,128)} %spectra_ref.1, s32[16,64]{1,0:T(8,128)} %bitcast.4), custom_call_target="tpu_custom_call" | custom-call | tf_op jit(solution)/shard_map/pallas_call | solution.py:42
  5.5 0.0 copy-start
  5.5 8.5 %all-to-all-start = ((bf16[32,80,128]{2,1,0:T(8,128)(2,1)}), bf16[32,80,128]{2,1,0:T(8,128)(2,1)S(1)}, u32[]{:S(2)}, u32[]{:S(2)}) async-start(bf16[32,80,128]{2,1,0:T(8,128)(2,1)} %shard_map.37), calls=%async_computation | async-start | bytes 1310720 | tf_op jit(solution)/shard_map/all_to_all | solution.py:151
  14.1 1.1 %fusion.4 = (f32[1,128,512]{2,1,0:T(8,128)S(1)}, f32[1,128,512]{2,1,0:T(8,128)S(1)}) fusion(s32[512]{0:T(512)S(1)} %iota_add_fusion, s32[128]{0:T(128)S(1)} %iota_add_fusion.1), kind=kLoop, calls=%fused_computation.14 | loop fusion | flops 983040 | bytes 526848 | tf_op jit(solution)/shard_map/cos | solution.py:140
  15.3 12.0 %all-to-all-done.x_ref = bf16[32,80,128]{2,1,0:T(8,128)(2,1)S(1)} async-done(((bf16[32,80,128]{2,1,0:T(8,128)(2,1)}), bf16[32,80,128]{2,1,0:T(8,128)(2,1)S(1)}, u32[]{:S(2)}, u32[]{:S(2)}) %all-to-all-start) | async-done | bytes 655392 | tf_op jit(solution)/shard_map/all_to_all | solution.py:151
  27.3 0.0 copy-done
  27.3 14.1 %shard_map.38 = bf16[256,512]{1,0:T(8,128)(2,1)} custom-call(s32[4]{0:T(128)S(1)} %copy-done, bf16[32,80,128]{2,1,0:T(8,128)(2,1)S(1)} %all-to-all-done.x_ref, bf16[256,512]{1,0:T(8,128)(2,1)S(1)} %bitcast.3), custom_call_target="tpu_custom_call" | custom-call | tf_op jit(solution)/shard_map/pallas_call | solution.py:119
  41.3 3.9 %all-to-all-start.1 = ((bf16[32,8,512]{2,1,0:T(8,128)(2,1)}), bf16[32,8,512]{2,1,0:T(8,128)(2,1)S(1)}, u32[]{:S(2)}, u32[]{:S(2)}) async-start(bf16[32,8,512]{2,1,0:T(8,128)(2,1)} %bitcast.2), calls=%async_computation.1 | async-start | bytes 524288 | tf_op jit(solution)/shard_map/all_to_all | solution.py:155
  45.2 0.5 convert_reduce_fusion
  45.7 8.4 %all-to-all-done.1 = bf16[32,8,512]{2,1,0:T(8,128)(2,1)S(1)} async-done(((bf16[32,8,512]{2,1,0:T(8,128)(2,1)}), bf16[32,8,512]{2,1,0:T(8,128)(2,1)S(1)}, u32[]{:S(2)}, u32[]{:S(2)}) %all-to-all-start.1) | async-done | bytes 262176 | tf_op jit(solution)/shard_map/all_to_all | solution.py:155
  54.2 2.8 %collective-permute-start.2 = (f32[8,512]{1,0:T(8,128)S(1)}, f32[8,512]{1,0:T(8,128)S(1)}, u32[]{:S(2)}, u32[]{:S(2)}) collective-permute-start(f32[8,512]{1,0:T(8,128)S(1)} %convert_reduce_fusion.1), channel_id=1, source_target_pairs={{0,3},{1,0},{2,1},{3,2},{4,7},{5,4},{6,5},{7,6},{8,11},{9,8},{10,9... | collective-permute-start | bytes 49160 | tf_op jit(solution)/shard_map/ppermute | solution.py:164
  57.0 0.8 %collective-permute-start.1 = (f32[8,512]{1,0:T(8,128)S(1)}, f32[8,512]{1,0:T(8,128)S(1)}, u32[]{:S(2)}, u32[]{:S(2)}) collective-permute-start(f32[8,512]{1,0:T(8,128)S(1)} %convert_reduce_fusion.1), channel_id=1, source_target_pairs={{0,2},{1,3},{2,0},{3,1},{4,6},{5,7},{6,4},{7,5},{8,10},{9,11},{10,... | collective-permute-start | bytes 49160 | tf_op jit(solution)/shard_map/ppermute | solution.py:164
  57.8 0.9 %collective-permute-start = (f32[8,512]{1,0:T(8,128)S(1)}, f32[8,512]{1,0:T(8,128)S(1)}, u32[]{:S(2)}, u32[]{:S(2)}) collective-permute-start(f32[8,512]{1,0:T(8,128)S(1)} %convert_reduce_fusion.1), channel_id=1, source_target_pairs={{0,1},{1,2},{2,3},{3,0},{4,5},{5,6},{6,7},{7,4},{8,9},{9,10},{10,1... | collective-permute-start | bytes 49160 | tf_op jit(solution)/shard_map/ppermute | solution.py:164
  58.7 0.0 collective-permute-done.2
  58.7 3.5 %collective-permute-done.1 = f32[8,512]{1,0:T(8,128)S(1)} collective-permute-done((f32[8,512]{1,0:T(8,128)S(1)}, f32[8,512]{1,0:T(8,128)S(1)}, u32[]{:S(2)}, u32[]{:S(2)}) %collective-permute-start.1) | collective-permute-done | bytes 16416 | tf_op jit(solution)/shard_map/ppermute | solution.py:164
  62.2 0.5 collective-permute-done
  62.7 0.7 %add_divide_fusion = f32[8,512]{1,0:T(8,128)} fusion(f32[8,512]{1,0:T(8,128)S(1)} %collective-permute-done.2, f32[8,512]{1,0:T(8,128)S(1)} %collective-permute-done.1, f32[8,512]{1,0:T(8,128)S(1)} %convert_reduce_fusion.1, f32[8,512]{1,0:T(8,128)S(1)} %collective-permute-done, f32[8]{0:T(128)S(1)} %multiply_sqrt_fusion), kind=kLoop, calls=%fused_computation.15 | loop fusion | flops 16384 | bytes 81952 | tf_op jit(solution)/shard_map/div | solution.py:167
  (7 shorter events, 0.1 us)
Async XLA Ops:
  5.5 21.8 %copy-start = (s32[4]{0:T(128)S(1)}, s32[4]{0:T(128)}, u32[]{:S(2)}) copy-start(s32[4]{0:T(128)} %plan_ref.1) | copy-start | bytes 52
  5.5 21.8 %all-to-all-start = ((bf16[32,80,128]{2,1,0:T(8,128)(2,1)}), bf16[32,80,128]{2,1,0:T(8,128)(2,1)S(1)}, u32[]{:S(2)}, u32[]{:S(2)}) async-start(bf16[32,80,128]{2,1,0:T(8,128)(2,1)} %shard_map.37), calls=%async_computation | async-start | bytes 1310720 | tf_op jit(solution)/shard_map/all_to_all | solution.py:151
  41.3 12.8 %all-to-all-start.1 = ((bf16[32,8,512]{2,1,0:T(8,128)(2,1)}), bf16[32,8,512]{2,1,0:T(8,128)(2,1)S(1)}, u32[]{:S(2)}, u32[]{:S(2)}) async-start(bf16[32,8,512]{2,1,0:T(8,128)(2,1)} %bitcast.2), calls=%async_computation.1 | async-start | bytes 524288 | tf_op jit(solution)/shard_map/all_to_all | solution.py:155
  54.2 4.5 %collective-permute-start.2 = (f32[8,512]{1,0:T(8,128)S(1)}, f32[8,512]{1,0:T(8,128)S(1)}, u32[]{:S(2)}, u32[]{:S(2)}) collective-permute-start(f32[8,512]{1,0:T(8,128)S(1)} %convert_reduce_fusion.1), channel_id=1, source_target_pairs={{0,3},{1,0},{2,1},{3,2},{4,7},{5,4},{6,5},{7,6},{8,11},{9,8},{10,9... | collective-permute-start | bytes 49160 | tf_op jit(solution)/shard_map/ppermute | solution.py:164
  57.0 5.2 %collective-permute-start.1 = (f32[8,512]{1,0:T(8,128)S(1)}, f32[8,512]{1,0:T(8,128)S(1)}, u32[]{:S(2)}, u32[]{:S(2)}) collective-permute-start(f32[8,512]{1,0:T(8,128)S(1)} %convert_reduce_fusion.1), channel_id=1, source_target_pairs={{0,2},{1,3},{2,0},{3,1},{4,6},{5,7},{6,4},{7,5},{8,10},{9,11},{10,... | collective-permute-start | bytes 49160 | tf_op jit(solution)/shard_map/ppermute | solution.py:164
  57.8 4.9 %collective-permute-start = (f32[8,512]{1,0:T(8,128)S(1)}, f32[8,512]{1,0:T(8,128)S(1)}, u32[]{:S(2)}, u32[]{:S(2)}) collective-permute-start(f32[8,512]{1,0:T(8,128)S(1)} %convert_reduce_fusion.1), channel_id=1, source_target_pairs={{0,1},{1,2},{2,3},{3,0},{4,5},{5,6},{6,7},{7,4},{8,9},{9,10},{10,1... | collective-permute-start | bytes 49160 | tf_op jit(solution)/shard_map/ppermute | solution.py:164

commit v2 on v1

--- a/solution.py
+++ b/solution.py
@@ -14,7 +14,7 @@
 NBINS = 256
 CH = 16
 SOURCES = STEPS * CH
-JBLK = 4
+JBLK = 16
 
 
 def whiten_kernel(spectra_ref, bins_ref, out_ref):
@@ -29,8 +29,9 @@
             imaginary = spectra_ref[w, 1, :, lanes]
             energy = real * real + imaginary * imaginary
             level = jnp.sqrt(jnp.mean(energy, axis=1, keepdims=True) + 1e-06)
-            out_ref[c, pl.ds(2 * w * CH, CH), :] = (real / level).astype(jnp.bfloat16)
-            out_ref[c, pl.ds((2 * w + 1) * CH, CH), :] = (imaginary / level).astype(jnp.bfloat16)
+            inverse = 1.0 / level
+            out_ref[c, pl.ds(2 * w * CH, CH), :] = (real * inverse).astype(jnp.bfloat16)
+            out_ref[c, pl.ds((2 * w + 1) * CH, CH), :] = (imaginary * inverse).astype(jnp.bfloat16)
         out_ref[c, pl.ds(2 * windows * CH, CH), :] = bins
 
 
@@ -38,7 +39,7 @@
     windows, _, channels, freq = spectra.shape
     owners = freq // BAND
     rows = 2 * windows * CH + CH
-    step = 4
+    step = 16
     return pl.pallas_call(
         whiten_kernel,
         grid=(owners // step,),
@@ -51,19 +52,47 @@
     )(spectra, bins)
 
 
+def hot_rows(bt_ref, j, channels):
+    numbers = lax.broadcasted_iota(jnp.int32, (NBINS, channels), 0).astype(jnp.float32)
+    named = jnp.broadcast_to(bt_ref[j][None], (NBINS // CH, CH, channels))
+    same = numbers.astype(jnp.bfloat16) == named.reshape(NBINS, channels)
+    return jnp.where(same, jnp.ones((), jnp.bfloat16), jnp.zeros((), jnp.bfloat16))
+
+
+def cross_piece(source, receiver, windows):
+    first = second = third = None
+    for w in range(windows):
+        products = [source[3 * w + p] * receiver[3 * w + p] for p in range(3)]
+        if first is None:
+            first, second, third = products
+        else:
+            first = first + products[0]
+            second = second + products[1]
+            third = third + products[2]
+    real = (first - third).astype(jnp.bfloat16)
+    imaginary = (first + second).astype(jnp.bfloat16)
+    return jnp.concatenate([real, imaginary], axis=1)
+
+
 def bin_kernel(windows, plan_ref, x_ref, table_ref, out_ref, rec_ref, src_ref, bt_ref, sums_ref):
     owners = x_ref.shape[0]
     channels = owners * CH
-    parts = 2 * windows
-    for p in range(parts):
-        rec_ref[p] = x_ref[:, pl.ds(p * CH, CH), :].reshape(channels, BAND)
+    for w in range(windows):
+        real = x_ref[:, pl.ds(2 * w * CH, CH), :].reshape(channels, BAND).astype(jnp.float32)
+        imaginary = x_ref[:, pl.ds((2 * w + 1) * CH, CH), :].reshape(channels, BAND)
+        imaginary = imaginary.astype(jnp.float32)
+        rec_ref[3 * w] = real
+        rec_ref[3 * w + 1] = -(real + imaginary)
+        rec_ref[3 * w + 2] = real - imaginary
     for q in range(STEPS):
-        for p in range(parts):
-            slab = x_ref[plan_ref[q], pl.ds(p * CH, CH), :].astype(jnp.float32)
-            for j in range(CH):
-                row = jnp.broadcast_to(slab[j:j + 1, :], (CH, BAND))
-                src_ref[q * CH + j, p] = row.astype(jnp.bfloat16)
-    bins = x_ref[:, pl.ds(parts * CH, CH), :].reshape(channels, BAND).astype(jnp.float32)
+        for w in range(windows):
+            real = x_ref[plan_ref[q], pl.ds(2 * w * CH, CH), :].astype(jnp.float32)
+            imaginary = x_ref[plan_ref[q], pl.ds((2 * w + 1) * CH, CH), :].astype(jnp.float32)
+            for p, value in enumerate((real + imaginary, real, imaginary)):
+                for j in range(CH):
+                    row = jnp.broadcast_to(value[j:j + 1, :], (8, BAND))
+                    src_ref[q * CH + j, 3 * w + p] = row
+    bins = x_ref[:, pl.ds(2 * windows * CH, CH), :].reshape(channels, BAND).astype(jnp.float32)
     turned = bins.T
     for j in range(SOURCES):
         row = jnp.broadcast_to(turned[j:j + 1, :], (CH, channels))
@@ -71,32 +100,17 @@
     sums_ref[...] = jnp.zeros_like(sums_ref)
 
     def step(index, carry):
-        numbers = lax.broadcasted_iota(jnp.int32, (NBINS, channels), 0).astype(jnp.float32)
-        numbers = numbers.astype(jnp.bfloat16)
-        one = jnp.ones((), jnp.bfloat16)
-        zero = jnp.zeros((), jnp.bfloat16)
         hots = []
         crosses = []
         for k in range(JBLK):
             j = index * JBLK + k
-            named = jnp.broadcast_to(bt_ref[j][None], (NBINS // CH, CH, channels))
-            hots.append(jnp.where(numbers == named.reshape(NBINS, channels), one, zero))
-            total_real = None
-            for w in range(windows):
-                sr = src_ref[j, 2 * w][None]
-                si = src_ref[j, 2 * w + 1][None]
-                rr = rec_ref[2 * w].reshape(owners, CH, BAND)
-                ri = rec_ref[2 * w + 1].reshape(owners, CH, BAND)
-                real = sr * rr + si * ri
-                imaginary = si * rr - sr * ri
-                if total_real is None:
-                    total_real, total_imaginary = real, imaginary
-                else:
-                    total_real = total_real + real
-                    total_imaginary = total_imaginary + imaginary
-            crosses.append(
-                jnp.concatenate([total_real, total_imaginary], axis=2).reshape(channels, 2 * BAND)
-            )
+            hots.append(hot_rows(bt_ref, j, channels))
+            source = [
+                jnp.concatenate([src_ref[j, p], src_ref[j, p]], axis=0) for p in range(3 * windows)
+            ]
+            for g in range(owners):
+                receiver = [rec_ref[p, pl.ds(g * CH, CH)] for p in range(3 * windows)]
+                crosses.append(cross_piece(source, receiver, windows))
         hot = jnp.concatenate(hots, axis=1)
         cross = jnp.concatenate(crosses, axis=0)
         sums_ref[...] += jnp.dot(hot, cross, preferred_element_type=jnp.float32)
@@ -122,8 +136,8 @@
         out_specs=vmem,
         out_shape=jax.ShapeDtypeStruct((NBINS, LAGS), jnp.bfloat16),
         scratch_shapes=[
-            pltpu.VMEM((2 * windows, channels, BAND), jnp.bfloat16),
-            pltpu.VMEM((SOURCES, 2 * windows, CH, BAND), jnp.bfloat16),
+            pltpu.VMEM((3 * windows, channels, BAND), jnp.float32),
+            pltpu.VMEM((SOURCES, 3 * windows, 8, BAND), jnp.float32),
             pltpu.VMEM((SOURCES, CH, channels), jnp.bfloat16),
             pltpu.VMEM((NBINS, 2 * BAND), jnp.float32),
         ],

time: 63.8 us -> 56.6 us (0.89)
  Pallas kernels: 19.6 us -> 12.5 us
    pallas_call x1, Pallas kernels: 14.1 us -> 10.3 us  [bin_sums(): pl.pallas_call(functools.partial(bin_kernel, windows), in_specs=[pl.Block...]
    pallas_call x1, Pallas kernels: 5.49 us -> 2.18 us  [whiten(): pl.pallas_call(whiten_kernel, grid=(owners // step,), in_specs=[pl.BlockS...]
where the time goes in v2:
time: 56.6 us; the launch traced here: 56.3 us
  waiting for transfers between devices  24.5 us (43%)
  starting transfers between devices  16.9 us (30%)
  Pallas kernels  12.5 us (22%)
  other arithmetic  2.38 us (4%)
    all_to_all x1, waiting for transfers between devices, per_device(): lax.all_to_all(outgoing, 'chan', split_axis=0, concat_axis=0, tiled=True)  12 us
    pallas_call x1, Pallas kernels, bin_sums(): pl.pallas_call(functools.partial(bin_kernel, windows), in_specs=[pl.Block...  10.3 us
    all_to_all x1, starting transfers between devices, per_device(): lax.all_to_all(outgoing, 'chan', split_axis=0, concat_axis=0, tiled=True)  8.55 us
    all_to_all x1, waiting for transfers between devices, per_device(): lax.all_to_all(partial.reshape(owners, bin_block, LAGS), 'chan', split_ax...  8.4 us
    ppermute x3, starting transfers between devices, per_device(): lax.ppermute(total, 'win', [(i, (i + d) % win_size) for i in range(win_si...  4.51 us
    ppermute x3, waiting for transfers between devices, per_device(): lax.ppermute(total, 'win', [(i, (i + d) % win_size) for i in range(win_si...  4.05 us
    all_to_all x1, starting transfers between devices, per_device(): lax.all_to_all(partial.reshape(owners, bin_block, LAGS), 'chan', split_ax...  3.87 us
    pallas_call x1, Pallas kernels, whiten(): pl.pallas_call(whiten_kernel, grid=(owners // step,), in_specs=[pl.BlockS...  2.18 us
  transfers between devices with their start and end apart: 5, of which 4 were waited for; matrix products, arithmetic and copies ran while one was open for 3% of the time, Pallas kernels for 0%

profile of v2, /device:TPU:0, one launch (start us, length us, event | category | flops | bytes accessed | tf_op | source)
XLA Modules:
  0.0 56.3 jit_solution(8006350467437374484)
XLA Ops:
  0.0 2.2 %shard_map.37 = bf16[32,80,128]{2,1,0:T(8,128)(2,1)} custom-call(f32[2,2,16,4096]{3,2,1,0:T(8,128)} %spectra_ref.1, s32[16,64]{1,0:T(8,128)} %bitcast.4), custom_call_target="tpu_custom_call" | custom-call | tf_op jit(solution)/shard_map/pallas_call | solution.py:43
  2.2 0.0 copy-start
  2.2 8.5 %all-to-all-start = ((bf16[32,80,128]{2,1,0:T(8,128)(2,1)}), bf16[32,80,128]{2,1,0:T(8,128)(2,1)S(1)}, u32[]{:S(2)}, u32[]{:S(2)}) async-start(bf16[32,80,128]{2,1,0:T(8,128)(2,1)} %shard_map.37), calls=%async_computation | async-start | bytes 1310720 | tf_op jit(solution)/shard_map/all_to_all | solution.py:165
  10.8 1.1 %fusion.4 = (f32[1,128,512]{2,1,0:T(8,128)S(1)}, f32[1,128,512]{2,1,0:T(8,128)S(1)}) fusion(s32[512]{0:T(512)S(1)} %iota_add_fusion, s32[128]{0:T(128)S(1)} %iota_add_fusion.1), kind=kLoop, calls=%fused_computation.14 | loop fusion | flops 983040 | bytes 526848 | tf_op jit(solution)/shard_map/cos | solution.py:154
  11.9 12.0 %all-to-all-done.x_ref = bf16[32,80,128]{2,1,0:T(8,128)(2,1)S(1)} async-done(((bf16[32,80,128]{2,1,0:T(8,128)(2,1)}), bf16[32,80,128]{2,1,0:T(8,128)(2,1)S(1)}, u32[]{:S(2)}, u32[]{:S(2)}) %all-to-all-start) | async-done | bytes 655392 | tf_op jit(solution)/shard_map/all_to_all | solution.py:165
  24.0 0.0 copy-done
  24.0 10.3 %shard_map.38 = bf16[256,512]{1,0:T(8,128)(2,1)} custom-call(s32[4]{0:T(128)S(1)} %copy-done, bf16[32,80,128]{2,1,0:T(8,128)(2,1)S(1)} %all-to-all-done.x_ref, bf16[256,512]{1,0:T(8,128)(2,1)S(1)} %bitcast.3), custom_call_target="tpu_custom_call" | custom-call | tf_op jit(solution)/shard_map/pallas_call | solution.py:133
  34.2 3.9 %all-to-all-start.1 = ((bf16[32,8,512]{2,1,0:T(8,128)(2,1)}), bf16[32,8,512]{2,1,0:T(8,128)(2,1)S(1)}, u32[]{:S(2)}, u32[]{:S(2)}) async-start(bf16[32,8,512]{2,1,0:T(8,128)(2,1)} %bitcast.2), calls=%async_computation.1 | async-start | bytes 524288 | tf_op jit(solution)/shard_map/all_to_all | solution.py:169
  38.1 0.5 convert_reduce_fusion
  38.6 8.4 %all-to-all-done.1 = bf16[32,8,512]{2,1,0:T(8,128)(2,1)S(1)} async-done(((bf16[32,8,512]{2,1,0:T(8,128)(2,1)}), bf16[32,8,512]{2,1,0:T(8,128)(2,1)S(1)}, u32[]{:S(2)}, u32[]{:S(2)}) %all-to-all-start.1) | async-done | bytes 262176 | tf_op jit(solution)/shard_map/all_to_all | solution.py:169
  47.1 2.8 %collective-permute-start.2 = (f32[8,512]{1,0:T(8,128)S(1)}, f32[8,512]{1,0:T(8,128)S(1)}, u32[]{:S(2)}, u32[]{:S(2)}) collective-permute-start(f32[8,512]{1,0:T(8,128)S(1)} %convert_reduce_fusion.1), channel_id=1, source_target_pairs={{0,3},{1,0},{2,1},{3,2},{4,7},{5,4},{6,5},{7,6},{8,11},{9,8},{10,9... | collective-permute-start | bytes 49160 | tf_op jit(solution)/shard_map/ppermute | solution.py:178
  49.9 0.8 %collective-permute-start.1 = (f32[8,512]{1,0:T(8,128)S(1)}, f32[8,512]{1,0:T(8,128)S(1)}, u32[]{:S(2)}, u32[]{:S(2)}) collective-permute-start(f32[8,512]{1,0:T(8,128)S(1)} %convert_reduce_fusion.1), channel_id=1, source_target_pairs={{0,2},{1,3},{2,0},{3,1},{4,6},{5,7},{6,4},{7,5},{8,10},{9,11},{10,... | collective-permute-start | bytes 49160 | tf_op jit(solution)/shard_map/ppermute | solution.py:178
  50.7 0.9 %collective-permute-start = (f32[8,512]{1,0:T(8,128)S(1)}, f32[8,512]{1,0:T(8,128)S(1)}, u32[]{:S(2)}, u32[]{:S(2)}) collective-permute-start(f32[8,512]{1,0:T(8,128)S(1)} %convert_reduce_fusion.1), channel_id=1, source_target_pairs={{0,1},{1,2},{2,3},{3,0},{4,5},{5,6},{6,7},{7,4},{8,9},{9,10},{10,1... | collective-permute-start | bytes 49160 | tf_op jit(solution)/shard_map/ppermute | solution.py:178
  51.6 0.0 collective-permute-done.2
  51.6 3.5 %collective-permute-done.1 = f32[8,512]{1,0:T(8,128)S(1)} collective-permute-done((f32[8,512]{1,0:T(8,128)S(1)}, f32[8,512]{1,0:T(8,128)S(1)}, u32[]{:S(2)}, u32[]{:S(2)}) %collective-permute-start.1) | collective-permute-done | bytes 16416 | tf_op jit(solution)/shard_map/ppermute | solution.py:178
  55.1 0.5 collective-permute-done
  55.6 0.7 %add_divide_fusion = f32[8,512]{1,0:T(8,128)} fusion(f32[8,512]{1,0:T(8,128)S(1)} %collective-permute-done.2, f32[8,512]{1,0:T(8,128)S(1)} %collective-permute-done.1, f32[8,512]{1,0:T(8,128)S(1)} %convert_reduce_fusion.1, f32[8,512]{1,0:T(8,128)S(1)} %collective-permute-done, f32[8]{0:T(128)S(1)} %multiply_sqrt_fusion), kind=kLoop, calls=%fused_computation.15 | loop fusion | flops 16384 | bytes 81952 | tf_op jit(solution)/shard_map/div | solution.py:181
  (7 shorter events, 0.1 us)
Async XLA Ops:
  2.2 21.8 %copy-start = (s32[4]{0:T(128)S(1)}, s32[4]{0:T(128)}, u32[]{:S(2)}) copy-start(s32[4]{0:T(128)} %plan_ref.1) | copy-start | bytes 52
  2.2 21.8 %all-to-all-start = ((bf16[32,80,128]{2,1,0:T(8,128)(2,1)}), bf16[32,80,128]{2,1,0:T(8,128)(2,1)S(1)}, u32[]{:S(2)}, u32[]{:S(2)}) async-start(bf16[32,80,128]{2,1,0:T(8,128)(2,1)} %shard_map.37), calls=%async_computation | async-start | bytes 1310720 | tf_op jit(solution)/shard_map/all_to_all | solution.py:165
  34.2 12.8 %all-to-all-start.1 = ((bf16[32,8,512]{2,1,0:T(8,128)(2,1)}), bf16[32,8,512]{2,1,0:T(8,128)(2,1)S(1)}, u32[]{:S(2)}, u32[]{:S(2)}) async-start(bf16[32,8,512]{2,1,0:T(8,128)(2,1)} %bitcast.2), calls=%async_computation.1 | async-start | bytes 524288 | tf_op jit(solution)/shard_map/all_to_all | solution.py:169
  47.1 4.5 %collective-permute-start.2 = (f32[8,512]{1,0:T(8,128)S(1)}, f32[8,512]{1,0:T(8,128)S(1)}, u32[]{:S(2)}, u32[]{:S(2)}) collective-permute-start(f32[8,512]{1,0:T(8,128)S(1)} %convert_reduce_fusion.1), channel_id=1, source_target_pairs={{0,3},{1,0},{2,1},{3,2},{4,7},{5,4},{6,5},{7,6},{8,11},{9,8},{10,9... | collective-permute-start | bytes 49160 | tf_op jit(solution)/shard_map/ppermute | solution.py:178
  49.9 5.2 %collective-permute-start.1 = (f32[8,512]{1,0:T(8,128)S(1)}, f32[8,512]{1,0:T(8,128)S(1)}, u32[]{:S(2)}, u32[]{:S(2)}) collective-permute-start(f32[8,512]{1,0:T(8,128)S(1)} %convert_reduce_fusion.1), channel_id=1, source_target_pairs={{0,2},{1,3},{2,0},{3,1},{4,6},{5,7},{6,4},{7,5},{8,10},{9,11},{10,... | collective-permute-start | bytes 49160 | tf_op jit(solution)/shard_map/ppermute | solution.py:178
  50.7 4.9 %collective-permute-start = (f32[8,512]{1,0:T(8,128)S(1)}, f32[8,512]{1,0:T(8,128)S(1)}, u32[]{:S(2)}, u32[]{:S(2)}) collective-permute-start(f32[8,512]{1,0:T(8,128)S(1)} %convert_reduce_fusion.1), channel_id=1, source_target_pairs={{0,1},{1,2},{2,3},{3,0},{4,5},{5,6},{6,7},{7,4},{8,9},{9,10},{10,1... | collective-permute-start | bytes 49160 | tf_op jit(solution)/shard_map/ppermute | solution.py:178

commit v3 on v2

--- a/solution.py
+++ b/solution.py
@@ -13,15 +13,16 @@
 STEPS = 4
 NBINS = 256
 CH = 16
+HALF = CH // 2
 SOURCES = STEPS * CH
-JBLK = 16
+JBLK = 32
 
 
 def whiten_kernel(spectra_ref, bins_ref, out_ref):
     chunks = out_ref.shape[0]
     windows = spectra_ref.shape[0]
     bins = bins_ref[...].astype(jnp.float32)
-    bins = jnp.concatenate([bins, jnp.zeros_like(bins)], axis=1).astype(jnp.bfloat16)
+    bins = jnp.concatenate([bins[:HALF], bins[HALF:]], axis=1).astype(jnp.bfloat16)
     for c in range(chunks):
         lanes = pl.ds(c * BAND, BAND)
         for w in range(windows):
@@ -32,13 +33,13 @@
             inverse = 1.0 / level
             out_ref[c, pl.ds(2 * w * CH, CH), :] = (real * inverse).astype(jnp.bfloat16)
             out_ref[c, pl.ds((2 * w + 1) * CH, CH), :] = (imaginary * inverse).astype(jnp.bfloat16)
-        out_ref[c, pl.ds(2 * windows * CH, CH), :] = bins
+        out_ref[c, pl.ds(2 * windows * CH, HALF), :] = bins
 
 
 def whiten(spectra, bins):
     windows, _, channels, freq = spectra.shape
     owners = freq // BAND
-    rows = 2 * windows * CH + CH
+    rows = 2 * windows * CH + HALF
     step = 16
     return pl.pallas_call(
         whiten_kernel,
@@ -48,7 +49,7 @@
             pl.BlockSpec(bins.shape, lambda i: (0, 0)),
         ],
         out_specs=pl.BlockSpec((step, rows, BAND), lambda i: (i, 0, 0)),
-        out_shape=jax.ShapeDtypeStruct((owners, rows, BAND), jnp.bfloat16),
+        out_shape=pltpu.VMEM((owners, rows, BAND), jnp.bfloat16),
     )(spectra, bins)
 
 
@@ -78,12 +79,15 @@
     owners = x_ref.shape[0]
     channels = owners * CH
     for w in range(windows):
-        real = x_ref[:, pl.ds(2 * w * CH, CH), :].reshape(channels, BAND).astype(jnp.float32)
-        imaginary = x_ref[:, pl.ds((2 * w + 1) * CH, CH), :].reshape(channels, BAND)
-        imaginary = imaginary.astype(jnp.float32)
-        rec_ref[3 * w] = real
-        rec_ref[3 * w + 1] = -(real + imaginary)
-        rec_ref[3 * w + 2] = real - imaginary
+        real_slabs = x_ref[:, pl.ds(2 * w * CH, CH), :].astype(jnp.float32)
+        imaginary_slabs = x_ref[:, pl.ds((2 * w + 1) * CH, CH), :].astype(jnp.float32)
+        for h in range(2):
+            rows = pl.ds(h * owners * HALF, owners * HALF)
+            real = real_slabs[:, h * HALF:(h + 1) * HALF].reshape(owners * HALF, BAND)
+            imaginary = imaginary_slabs[:, h * HALF:(h + 1) * HALF].reshape(owners * HALF, BAND)
+            rec_ref[3 * w, rows] = real
+            rec_ref[3 * w + 1, rows] = -(real + imaginary)
+            rec_ref[3 * w + 2, rows] = real - imaginary
     for q in range(STEPS):
         for w in range(windows):
             real = x_ref[plan_ref[q], pl.ds(2 * w * CH, CH), :].astype(jnp.float32)
@@ -92,11 +96,11 @@
                 for j in range(CH):
                     row = jnp.broadcast_to(value[j:j + 1, :], (8, BAND))
                     src_ref[q * CH + j, 3 * w + p] = row
-    bins = x_ref[:, pl.ds(2 * windows * CH, CH), :].reshape(channels, BAND).astype(jnp.float32)
-    turned = bins.T
+    bins = x_ref[:, pl.ds(2 * windows * CH, HALF), :].astype(jnp.float32)
+    turned = bins.reshape(owners * HALF, BAND).T
     for j in range(SOURCES):
-        row = jnp.broadcast_to(turned[j:j + 1, :], (CH, channels))
-        bt_ref[j] = row.astype(jnp.bfloat16)
+        row = jnp.concatenate([turned[j:j + 1], turned[SOURCES + j:SOURCES + j + 1]], axis=1)
+        bt_ref[j] = jnp.broadcast_to(row, (CH, channels)).astype(jnp.bfloat16)
     sums_ref[...] = jnp.zeros_like(sums_ref)
 
     def step(index, carry):
@@ -134,7 +138,7 @@
         functools.partial(bin_kernel, windows),
         in_specs=[pl.BlockSpec(memory_space=pltpu.SMEM), vmem, vmem],
         out_specs=vmem,
-        out_shape=jax.ShapeDtypeStruct((NBINS, LAGS), jnp.bfloat16),
+        out_shape=pltpu.VMEM((NBINS, LAGS), jnp.bfloat16),
         scratch_shapes=[
             pltpu.VMEM((3 * windows, channels, BAND), jnp.float32),
             pltpu.VMEM((SOURCES, 3 * windows, 8, BAND), jnp.float32),
@@ -170,7 +174,7 @@
         partial.reshape(owners, bin_block, LAGS), "chan", split_axis=0, concat_axis=0, tiled=True
     )
     total = jnp.sum(arrived.astype(jnp.float32), axis=0)
-    named = gathered[:, 2 * windows * CH:, :SOURCES].astype(jnp.float32)
+    named = gathered[:, 2 * windows * CH:].astype(jnp.float32)
     mine = (own * bin_block + lax.iota(jnp.int32, bin_block)).astype(jnp.float32)
     counts = jnp.sum((named[None] == mine[:, None, None, None]).astype(jnp.float32), axis=(1, 2, 3))
     summed = total

time: 56.6 us -> 55.4 us (0.979)
    all_to_all x1, waiting for transfers between devices: 12 us -> 11.3 us  [per_device(): lax.all_to_all(outgoing, 'chan', split_axis=0, concat_axis=0, tiled=True)]
where the time goes in v3:
time: 55.4 us; the launch traced here: 55.1 us
  waiting for transfers between devices  24 us (43%)
  starting transfers between devices  16.8 us (30%)
  Pallas kernels  12.1 us (22%)
  other arithmetic  2.17 us (4%)
    all_to_all x1, waiting for transfers between devices, per_device(): lax.all_to_all(outgoing, 'chan', split_axis=0, concat_axis=0, tiled=True)  11.3 us
    pallas_call x1, Pallas kernels, bin_sums(): pl.pallas_call(functools.partial(bin_kernel, windows), in_specs=[pl.Block...  9.87 us
    all_to_all x1, waiting for transfers between devices, per_device(): lax.all_to_all(partial.reshape(owners, bin_block, LAGS), 'chan', split_ax...  8.61 us
    all_to_all x1, starting transfers between devices, per_device(): lax.all_to_all(outgoing, 'chan', split_axis=0, concat_axis=0, tiled=True)  8.42 us
    ppermute x3, starting transfers between devices, per_device(): lax.ppermute(total, 'win', [(i, (i + d) % win_size) for i in range(win_si...  4.51 us
    ppermute x3, waiting for transfers between devices, per_device(): lax.ppermute(total, 'win', [(i, (i + d) % win_size) for i in range(win_si...  4.06 us
    all_to_all x1, starting transfers between devices, per_device(): lax.all_to_all(partial.reshape(owners, bin_block, LAGS), 'chan', split_ax...  3.87 us
    pallas_call x1, Pallas kernels, whiten(): pl.pallas_call(whiten_kernel, grid=(owners // step,), in_specs=[pl.BlockS...  2.2 us
  transfers between devices with their start and end apart: 5, of which 4 were waited for; matrix products, arithmetic and copies ran while one was open for 3% of the time, Pallas kernels for 0%

profile of v3, /device:TPU:0, one launch (start us, length us, event | category | flops | bytes accessed | tf_op | source)
XLA Modules:
  0.0 55.1 jit_solution(6092297322350653390)
XLA Ops:
  0.0 2.2 %shard_map.37 = bf16[32,72,128]{2,1,0:T(8,128)(2,1)} custom-call(f32[2,2,16,4096]{3,2,1,0:T(8,128)} %spectra_ref.1, s32[16,64]{1,0:T(8,128)} %bitcast.4), custom_call_target="tpu_custom_call" | custom-call | tf_op jit(solution)/shard_map/pallas_call | solution.py:44
  2.2 8.4 %all-to-all-start = ((bf16[32,72,128]{2,1,0:T(8,128)(2,1)}), bf16[32,72,128]{2,1,0:T(8,128)(2,1)S(1)}, u32[]{:S(2)}, u32[]{:S(2)}) async-start(bf16[32,72,128]{2,1,0:T(8,128)(2,1)} %shard_map.37), calls=%async_computation | async-start | bytes 1179648 | tf_op jit(solution)/shard_map/all_to_all | solution.py:169
  10.7 1.1 %fusion.4 = (f32[1,128,512]{2,1,0:T(8,128)S(1)}, f32[1,128,512]{2,1,0:T(8,128)S(1)}) fusion(s32[512]{0:T(512)S(1)} %iota_add_fusion, s32[128]{0:T(128)S(1)} %iota_add_fusion.1), kind=kLoop, calls=%fused_computation.13 | loop fusion | flops 983040 | bytes 526848 | tf_op jit(solution)/shard_map/cos | solution.py:158
  11.8 0.0 copy-start
  11.8 11.3 %all-to-all-done.x_ref = bf16[32,72,128]{2,1,0:T(8,128)(2,1)S(1)} async-done(((bf16[32,72,128]{2,1,0:T(8,128)(2,1)}), bf16[32,72,128]{2,1,0:T(8,128)(2,1)S(1)}, u32[]{:S(2)}, u32[]{:S(2)}) %all-to-all-start) | async-done | bytes 589856 | tf_op jit(solution)/shard_map/all_to_all | solution.py:169
  23.2 0.0 copy-done
  23.2 9.9 %shard_map.38 = bf16[256,512]{1,0:T(8,128)(2,1)} custom-call(s32[4]{0:T(128)S(1)} %copy-done, bf16[32,72,128]{2,1,0:T(8,128)(2,1)S(1)} %all-to-all-done.x_ref, bf16[256,512]{1,0:T(8,128)(2,1)S(1)} %bitcast.3), custom_call_target="tpu_custom_call" | custom-call | tf_op jit(solution)/shard_map/pallas_call | solution.py:137
  33.0 3.9 %all-to-all-start.1 = ((bf16[32,8,512]{2,1,0:T(8,128)(2,1)}), bf16[32,8,512]{2,1,0:T(8,128)(2,1)S(1)}, u32[]{:S(2)}, u32[]{:S(2)}) async-start(bf16[32,8,512]{2,1,0:T(8,128)(2,1)} %bitcast.2), calls=%async_computation.1 | async-start | bytes 524288 | tf_op jit(solution)/shard_map/all_to_all | solution.py:173
  36.9 0.3 convert_reduce_fusion
  37.2 8.6 %all-to-all-done.1 = bf16[32,8,512]{2,1,0:T(8,128)(2,1)S(1)} async-done(((bf16[32,8,512]{2,1,0:T(8,128)(2,1)}), bf16[32,8,512]{2,1,0:T(8,128)(2,1)S(1)}, u32[]{:S(2)}, u32[]{:S(2)}) %all-to-all-start.1) | async-done | bytes 262176 | tf_op jit(solution)/shard_map/all_to_all | solution.py:173
  45.8 2.8 %collective-permute-start.2 = (f32[8,512]{1,0:T(8,128)S(1)}, f32[8,512]{1,0:T(8,128)S(1)}, u32[]{:S(2)}, u32[]{:S(2)}) collective-permute-start(f32[8,512]{1,0:T(8,128)S(1)} %convert_reduce_fusion.1), channel_id=1, source_target_pairs={{0,3},{1,0},{2,1},{3,2},{4,7},{5,4},{6,5},{7,6},{8,11},{9,8},{10,9... | collective-permute-start | bytes 49160 | tf_op jit(solution)/shard_map/ppermute | solution.py:182
  48.7 0.8 %collective-permute-start.1 = (f32[8,512]{1,0:T(8,128)S(1)}, f32[8,512]{1,0:T(8,128)S(1)}, u32[]{:S(2)}, u32[]{:S(2)}) collective-permute-start(f32[8,512]{1,0:T(8,128)S(1)} %convert_reduce_fusion.1), channel_id=1, source_target_pairs={{0,2},{1,3},{2,0},{3,1},{4,6},{5,7},{6,4},{7,5},{8,10},{9,11},{10,... | collective-permute-start | bytes 49160 | tf_op jit(solution)/shard_map/ppermute | solution.py:182
  49.5 0.9 %collective-permute-start = (f32[8,512]{1,0:T(8,128)S(1)}, f32[8,512]{1,0:T(8,128)S(1)}, u32[]{:S(2)}, u32[]{:S(2)}) collective-permute-start(f32[8,512]{1,0:T(8,128)S(1)} %convert_reduce_fusion.1), channel_id=1, source_target_pairs={{0,1},{1,2},{2,3},{3,0},{4,5},{5,6},{6,7},{7,4},{8,9},{9,10},{10,1... | collective-permute-start | bytes 49160 | tf_op jit(solution)/shard_map/ppermute | solution.py:182
  50.4 0.0 collective-permute-done.2
  50.4 3.5 %collective-permute-done.1 = f32[8,512]{1,0:T(8,128)S(1)} collective-permute-done((f32[8,512]{1,0:T(8,128)S(1)}, f32[8,512]{1,0:T(8,128)S(1)}, u32[]{:S(2)}, u32[]{:S(2)}) %collective-permute-start.1) | collective-permute-done | bytes 16416 | tf_op jit(solution)/shard_map/ppermute | solution.py:182
  53.9 0.5 collective-permute-done
  54.4 0.7 %add_divide_fusion = f32[8,512]{1,0:T(8,128)} fusion(f32[8,512]{1,0:T(8,128)S(1)} %collective-permute-done.2, f32[8,512]{1,0:T(8,128)S(1)} %collective-permute-done.1, f32[8,512]{1,0:T(8,128)S(1)} %convert_reduce_fusion.1, f32[8,512]{1,0:T(8,128)S(1)} %collective-permute-done, f32[8]{0:T(128)S(1)} %multiply_sqrt_fusion), kind=kLoop, calls=%fused_computation.15 | loop fusion | flops 16384 | bytes 81952 | tf_op jit(solution)/shard_map/div | solution.py:185
  (7 shorter events, 0.1 us)
Async XLA Ops:
  2.2 21.0 %all-to-all-start = ((bf16[32,72,128]{2,1,0:T(8,128)(2,1)}), bf16[32,72,128]{2,1,0:T(8,128)(2,1)S(1)}, u32[]{:S(2)}, u32[]{:S(2)}) async-start(bf16[32,72,128]{2,1,0:T(8,128)(2,1)} %shard_map.37), calls=%async_computation | async-start | bytes 1179648 | tf_op jit(solution)/shard_map/all_to_all | solution.py:169
  11.8 11.3 %copy-start = (s32[4]{0:T(128)S(1)}, s32[4]{0:T(128)}, u32[]{:S(2)}) copy-start(s32[4]{0:T(128)} %plan_ref.1) | copy-start | bytes 52
  33.0 12.8 %all-to-all-start.1 = ((bf16[32,8,512]{2,1,0:T(8,128)(2,1)}), bf16[32,8,512]{2,1,0:T(8,128)(2,1)S(1)}, u32[]{:S(2)}, u32[]{:S(2)}) async-start(bf16[32,8,512]{2,1,0:T(8,128)(2,1)} %bitcast.2), calls=%async_computation.1 | async-start | bytes 524288 | tf_op jit(solution)/shard_map/all_to_all | solution.py:173
  45.8 4.5 %collective-permute-start.2 = (f32[8,512]{1,0:T(8,128)S(1)}, f32[8,512]{1,0:T(8,128)S(1)}, u32[]{:S(2)}, u32[]{:S(2)}) collective-permute-start(f32[8,512]{1,0:T(8,128)S(1)} %convert_reduce_fusion.1), channel_id=1, source_target_pairs={{0,3},{1,0},{2,1},{3,2},{4,7},{5,4},{6,5},{7,6},{8,11},{9,8},{10,9... | collective-permute-start | bytes 49160 | tf_op jit(solution)/shard_map/ppermute | solution.py:182
  48.7 5.2 %collective-permute-start.1 = (f32[8,512]{1,0:T(8,128)S(1)}, f32[8,512]{1,0:T(8,128)S(1)}, u32[]{:S(2)}, u32[]{:S(2)}) collective-permute-start(f32[8,512]{1,0:T(8,128)S(1)} %convert_reduce_fusion.1), channel_id=1, source_target_pairs={{0,2},{1,3},{2,0},{3,1},{4,6},{5,7},{6,4},{7,5},{8,10},{9,11},{10,... | collective-permute-start | bytes 49160 | tf_op jit(solution)/shard_map/ppermute | solution.py:182
  49.5 4.9 %collective-permute-start = (f32[8,512]{1,0:T(8,128)S(1)}, f32[8,512]{1,0:T(8,128)S(1)}, u32[]{:S(2)}, u32[]{:S(2)}) collective-permute-start(f32[8,512]{1,0:T(8,128)S(1)} %convert_reduce_fusion.1), channel_id=1, source_target_pairs={{0,1},{1,2},{2,3},{3,0},{4,5},{5,6},{6,7},{7,4},{8,9},{9,10},{10,1... | collective-permute-start | bytes 49160 | tf_op jit(solution)/shard_map/ppermute | solution.py:182

commit v4 on v3

--- a/solution.py
+++ b/solution.py
@@ -29,8 +29,7 @@
             real = spectra_ref[w, 0, :, lanes]
             imaginary = spectra_ref[w, 1, :, lanes]
             energy = real * real + imaginary * imaginary
-            level = jnp.sqrt(jnp.mean(energy, axis=1, keepdims=True) + 1e-06)
-            inverse = 1.0 / level
+            inverse = lax.rsqrt(jnp.mean(energy, axis=1, keepdims=True) + 1e-06)
             out_ref[c, pl.ds(2 * w * CH, CH), :] = (real * inverse).astype(jnp.bfloat16)
             out_ref[c, pl.ds((2 * w + 1) * CH, CH), :] = (imaginary * inverse).astype(jnp.bfloat16)
         out_ref[c, pl.ds(2 * windows * CH, HALF), :] = bins
@@ -125,8 +124,10 @@
     high = sums.astype(jnp.bfloat16)
     low = (sums - high.astype(jnp.float32)).astype(jnp.bfloat16)
     table = table_ref[...]
-    lags = jnp.dot(high, table, preferred_element_type=jnp.float32)
-    lags = lags + jnp.dot(low, table, preferred_element_type=jnp.float32)
+    both = jnp.concatenate([high, low], axis=1)
+    lags = jnp.dot(
+        both, jnp.concatenate([table, table], axis=0), preferred_element_type=jnp.float32
+    )
     out_ref[...] = lags.astype(jnp.bfloat16)
 
 
@@ -177,12 +178,14 @@
     named = gathered[:, 2 * windows * CH:].astype(jnp.float32)
     mine = (own * bin_block + lax.iota(jnp.int32, bin_block)).astype(jnp.float32)
     counts = jnp.sum((named[None] == mine[:, None, None, None]).astype(jnp.float32), axis=(1, 2, 3))
-    summed = total
+    scale = 1.0 / jnp.sqrt(counts * (windows * win_size))
+    scaled = total * scale[:, None]
+    sent = scaled
+    summed = scaled
     for d in range(1, win_size):
-        summed = summed + lax.ppermute(
-            total, "win", [(i, (i + d) % win_size) for i in range(win_size)]
-        )
-    return summed / jnp.sqrt(counts * (windows * win_size))[:, None]
+        passed = lax.ppermute(sent, "win", [(i, (i + d) % win_size) for i in range(win_size)])
+        summed = summed + passed
+    return summed
 
 
 def solution(mesh):

time: 55.4 us -> 55.3 us (level)
    div x1 -> x0, other arithmetic: 0.68 us -> none  [per_device(): return summed / jnp.sqrt(counts * (windows * win_size))[:, None]]
    add x0 -> x1, other arithmetic: none -> 0.68 us  [per_device(): summed = summed + passed]
where the time goes in v4:
time: 55.3 us; the launch traced here: 55 us
  waiting for transfers between devices  24 us (43%)
  starting transfers between devices  16.7 us (30%)
  Pallas kernels  12 us (22%)
  other arithmetic  2.24 us (4%)
    all_to_all x1, waiting for transfers between devices, per_device(): lax.all_to_all(outgoing, 'chan', split_axis=0, concat_axis=0, tiled=True)  11.3 us
    pallas_call x1, Pallas kernels, bin_sums(): pl.pallas_call(functools.partial(bin_kernel, windows), in_specs=[pl.Block...  9.87 us
    all_to_all x1, waiting for transfers between devices, per_device(): lax.all_to_all(partial.reshape(owners, bin_block, LAGS), 'chan', split_ax...  8.6 us
    all_to_all x1, starting transfers between devices, per_device(): lax.all_to_all(outgoing, 'chan', split_axis=0, concat_axis=0, tiled=True)  8.42 us
    ppermute x3, starting transfers between devices, per_device(): lax.ppermute(sent, 'win', [(i, (i + d) % win_size) for i in range(win_siz...  4.45 us
    ppermute x3, waiting for transfers between devices, per_device(): lax.ppermute(sent, 'win', [(i, (i + d) % win_size) for i in range(win_siz...  4.06 us
    all_to_all x1, starting transfers between devices, per_device(): lax.all_to_all(partial.reshape(owners, bin_block, LAGS), 'chan', split_ax...  3.87 us
    pallas_call x1, Pallas kernels, whiten(): pl.pallas_call(whiten_kernel, grid=(owners // step,), in_specs=[pl.BlockS...  2.1 us
  transfers between devices with their start and end apart: 5, of which 4 were waited for; matrix products, arithmetic and copies ran while one was open for 3% of the time, Pallas kernels for 0%

profile of v4, /device:TPU:0, one launch (start us, length us, event | category | flops | bytes accessed | tf_op | source)
XLA Modules:
  0.0 55.0 jit_solution(10332409159644269962)
XLA Ops:
  0.0 2.1 %shard_map.37 = bf16[32,72,128]{2,1,0:T(8,128)(2,1)} custom-call(f32[2,2,16,4096]{3,2,1,0:T(8,128)} %spectra_ref.1, s32[16,64]{1,0:T(8,128)} %bitcast.4), custom_call_target="tpu_custom_call" | custom-call | tf_op jit(solution)/shard_map/pallas_call | solution.py:43
  2.1 8.4 %all-to-all-start = ((bf16[32,72,128]{2,1,0:T(8,128)(2,1)}), bf16[32,72,128]{2,1,0:T(8,128)(2,1)S(1)}, u32[]{:S(2)}, u32[]{:S(2)}) async-start(bf16[32,72,128]{2,1,0:T(8,128)(2,1)} %shard_map.37), calls=%async_computation | async-start | bytes 1179648 | tf_op jit(solution)/shard_map/all_to_all | solution.py:170
  10.6 1.1 %fusion.4 = (f32[1,128,512]{2,1,0:T(8,128)S(1)}, f32[1,128,512]{2,1,0:T(8,128)S(1)}) fusion(s32[512]{0:T(512)S(1)} %iota_add_fusion, s32[128]{0:T(128)S(1)} %iota_add_fusion.1), kind=kLoop, calls=%fused_computation.13 | loop fusion | flops 983040 | bytes 526848 | tf_op jit(solution)/shard_map/cos | solution.py:159
  11.7 0.0 copy-start
  11.7 11.3 %all-to-all-done.x_ref = bf16[32,72,128]{2,1,0:T(8,128)(2,1)S(1)} async-done(((bf16[32,72,128]{2,1,0:T(8,128)(2,1)}), bf16[32,72,128]{2,1,0:T(8,128)(2,1)S(1)}, u32[]{:S(2)}, u32[]{:S(2)}) %all-to-all-start) | async-done | bytes 589856 | tf_op jit(solution)/shard_map/all_to_all | solution.py:170
  23.1 0.0 copy-done
  23.1 9.9 %shard_map.38 = bf16[256,512]{1,0:T(8,128)(2,1)} custom-call(s32[4]{0:T(128)S(1)} %copy-done, bf16[32,72,128]{2,1,0:T(8,128)(2,1)S(1)} %all-to-all-done.x_ref, bf16[256,512]{1,0:T(8,128)(2,1)S(1)} %bitcast.3), custom_call_target="tpu_custom_call" | custom-call | tf_op jit(solution)/shard_map/pallas_call | solution.py:138
  32.9 3.9 %all-to-all-start.1 = ((bf16[32,8,512]{2,1,0:T(8,128)(2,1)}), bf16[32,8,512]{2,1,0:T(8,128)(2,1)S(1)}, u32[]{:S(2)}, u32[]{:S(2)}) async-start(bf16[32,8,512]{2,1,0:T(8,128)(2,1)} %bitcast.2), calls=%async_computation.1 | async-start | bytes 524288 | tf_op jit(solution)/shard_map/all_to_all | solution.py:174
  36.8 0.3 convert_reduce_fusion
  37.1 8.6 %all-to-all-done.1 = bf16[32,8,512]{2,1,0:T(8,128)(2,1)S(1)} async-done(((bf16[32,8,512]{2,1,0:T(8,128)(2,1)}), bf16[32,8,512]{2,1,0:T(8,128)(2,1)S(1)}, u32[]{:S(2)}, u32[]{:S(2)}) %all-to-all-start.1) | async-done | bytes 262176 | tf_op jit(solution)/shard_map/all_to_all | solution.py:174
  45.8 0.1 broadcast_multiply_fusion
  45.8 2.8 %collective-permute-start.2 = (f32[8,512]{1,0:T(8,128)S(1)}, f32[8,512]{1,0:T(8,128)S(1)}, u32[]{:S(2)}, u32[]{:S(2)}) collective-permute-start(f32[8,512]{1,0:T(8,128)S(1)} %broadcast_multiply_fusion), channel_id=1, source_target_pairs={{0,3},{1,0},{2,1},{3,2},{4,7},{5,4},{6,5},{7,6},{8,11},{9,8},{10,9... | collective-permute-start | bytes 49160 | tf_op jit(solution)/shard_map/ppermute | solution.py:186
  48.6 0.8 %collective-permute-start.1 = (f32[8,512]{1,0:T(8,128)S(1)}, f32[8,512]{1,0:T(8,128)S(1)}, u32[]{:S(2)}, u32[]{:S(2)}) collective-permute-start(f32[8,512]{1,0:T(8,128)S(1)} %broadcast_multiply_fusion), channel_id=1, source_target_pairs={{0,2},{1,3},{2,0},{3,1},{4,6},{5,7},{6,4},{7,5},{8,10},{9,11},{10,... | collective-permute-start | bytes 49160 | tf_op jit(solution)/shard_map/ppermute | solution.py:186
  49.4 0.9 %collective-permute-start = (f32[8,512]{1,0:T(8,128)S(1)}, f32[8,512]{1,0:T(8,128)S(1)}, u32[]{:S(2)}, u32[]{:S(2)}) collective-permute-start(f32[8,512]{1,0:T(8,128)S(1)} %broadcast_multiply_fusion), channel_id=1, source_target_pairs={{0,1},{1,2},{2,3},{3,0},{4,5},{5,6},{6,7},{7,4},{8,9},{9,10},{10,1... | collective-permute-start | bytes 49160 | tf_op jit(solution)/shard_map/ppermute | solution.py:186
  50.3 0.0 collective-permute-done.2
  50.3 3.6 %collective-permute-done.1 = f32[8,512]{1,0:T(8,128)S(1)} collective-permute-done((f32[8,512]{1,0:T(8,128)S(1)}, f32[8,512]{1,0:T(8,128)S(1)}, u32[]{:S(2)}, u32[]{:S(2)}) %collective-permute-start.1) | collective-permute-done | bytes 16416 | tf_op jit(solution)/shard_map/ppermute | solution.py:186
  53.8 0.5 collective-permute-done
  54.3 0.7 %add_add_fusion = f32[8,512]{1,0:T(8,128)} fusion(f32[8,512]{1,0:T(8,128)S(1)} %collective-permute-done.2, f32[8,512]{1,0:T(8,128)S(1)} %collective-permute-done.1, f32[8,512]{1,0:T(8,128)S(1)} %collective-permute-done, f32[8,512]{1,0:T(8,128)S(1)} %convert_reduce_fusion.1, f32[8]{0:T(128)S(1)} %multiply_rsqrt_fusion), kind=kLoop, calls=%fused_computation.15 | loop fusion | flops 16384 | bytes 81952 | tf_op jit(solution)/shard_map/add | solution.py:187
  (7 shorter events, 0.1 us)
Async XLA Ops:
  2.1 21.0 %all-to-all-start = ((bf16[32,72,128]{2,1,0:T(8,128)(2,1)}), bf16[32,72,128]{2,1,0:T(8,128)(2,1)S(1)}, u32[]{:S(2)}, u32[]{:S(2)}) async-start(bf16[32,72,128]{2,1,0:T(8,128)(2,1)} %shard_map.37), calls=%async_computation | async-start | bytes 1179648 | tf_op jit(solution)/shard_map/all_to_all | solution.py:170
  11.7 11.3 %copy-start = (s32[4]{0:T(128)S(1)}, s32[4]{0:T(128)}, u32[]{:S(2)}) copy-start(s32[4]{0:T(128)} %plan_ref.1) | copy-start | bytes 52
  32.9 12.8 %all-to-all-start.1 = ((bf16[32,8,512]{2,1,0:T(8,128)(2,1)}), bf16[32,8,512]{2,1,0:T(8,128)(2,1)S(1)}, u32[]{:S(2)}, u32[]{:S(2)}) async-start(bf16[32,8,512]{2,1,0:T(8,128)(2,1)} %bitcast.2), calls=%async_computation.1 | async-start | bytes 524288 | tf_op jit(solution)/shard_map/all_to_all | solution.py:174
  45.8 4.5 %collective-permute-start.2 = (f32[8,512]{1,0:T(8,128)S(1)}, f32[8,512]{1,0:T(8,128)S(1)}, u32[]{:S(2)}, u32[]{:S(2)}) collective-permute-start(f32[8,512]{1,0:T(8,128)S(1)} %broadcast_multiply_fusion), channel_id=1, source_target_pairs={{0,3},{1,0},{2,1},{3,2},{4,7},{5,4},{6,5},{7,6},{8,11},{9,8},{10,9... | collective-permute-start | bytes 49160 | tf_op jit(solution)/shard_map/ppermute | solution.py:186
  48.6 5.2 %collective-permute-start.1 = (f32[8,512]{1,0:T(8,128)S(1)}, f32[8,512]{1,0:T(8,128)S(1)}, u32[]{:S(2)}, u32[]{:S(2)}) collective-permute-start(f32[8,512]{1,0:T(8,128)S(1)} %broadcast_multiply_fusion), channel_id=1, source_target_pairs={{0,2},{1,3},{2,0},{3,1},{4,6},{5,7},{6,4},{7,5},{8,10},{9,11},{10,... | collective-permute-start | bytes 49160 | tf_op jit(solution)/shard_map/ppermute | solution.py:186
  49.4 4.9 %collective-permute-start = (f32[8,512]{1,0:T(8,128)S(1)}, f32[8,512]{1,0:T(8,128)S(1)}, u32[]{:S(2)}, u32[]{:S(2)}) collective-permute-start(f32[8,512]{1,0:T(8,128)S(1)} %broadcast_multiply_fusion), channel_id=1, source_target_pairs={{0,1},{1,2},{2,3},{3,0},{4,5},{5,6},{6,7},{7,4},{8,9},{9,10},{10,1... | collective-permute-start | bytes 49160 | tf_op jit(solution)/shard_map/ppermute | solution.py:186

commit v5 on v3

--- a/solution.py
+++ b/solution.py
@@ -125,8 +125,9 @@
     high = sums.astype(jnp.bfloat16)
     low = (sums - high.astype(jnp.float32)).astype(jnp.bfloat16)
     table = table_ref[...]
-    lags = jnp.dot(high, table, preferred_element_type=jnp.float32)
-    lags = lags + jnp.dot(low, table, preferred_element_type=jnp.float32)
+    both = jnp.concatenate([high, low], axis=1)
+    tables = jnp.concatenate([table, table], axis=0)
+    lags = jnp.dot(both, tables, preferred_element_type=jnp.float32)
     out_ref[...] = lags.astype(jnp.bfloat16)
 
 

time: 55.4 us -> 55.4 us (level)
  no operation moved by 1% of the time
where the time goes in v5:
time: 55.4 us; the launch traced here: 55.1 us
  waiting for transfers between devices  24 us (43%)
  starting transfers between devices  16.8 us (30%)
  Pallas kernels  12.1 us (22%)
  other arithmetic  2.17 us (4%)
    all_to_all x1, waiting for transfers between devices, per_device(): lax.all_to_all(outgoing, 'chan', split_axis=0, concat_axis=0, tiled=True)  11.3 us
    pallas_call x1, Pallas kernels, bin_sums(): pl.pallas_call(functools.partial(bin_kernel, windows), in_specs=[pl.Block...  9.87 us
    all_to_all x1, waiting for transfers between devices, per_device(): lax.all_to_all(partial.reshape(owners, bin_block, LAGS), 'chan', split_ax...  8.61 us
    all_to_all x1, starting transfers between devices, per_device(): lax.all_to_all(outgoing, 'chan', split_axis=0, concat_axis=0, tiled=True)  8.42 us
    ppermute x3, starting transfers between devices, per_device(): lax.ppermute(total, 'win', [(i, (i + d) % win_size) for i in range(win_si...  4.51 us
    ppermute x3, waiting for transfers between devices, per_device(): lax.ppermute(total, 'win', [(i, (i + d) % win_size) for i in range(win_si...  4.06 us
    all_to_all x1, starting transfers between devices, per_device(): lax.all_to_all(partial.reshape(owners, bin_block, LAGS), 'chan', split_ax...  3.87 us
    pallas_call x1, Pallas kernels, whiten(): pl.pallas_call(whiten_kernel, grid=(owners // step,), in_specs=[pl.BlockS...  2.2 us
  transfers between devices with their start and end apart: 5, of which 4 were waited for; matrix products, arithmetic and copies ran while one was open for 3% of the time, Pallas kernels for 0%

profile of v5, /device:TPU:0, one launch (start us, length us, event | category | flops | bytes accessed | tf_op | source)
XLA Modules:
  0.0 55.1 jit_solution(8730824071815122344)
XLA Ops:
  0.0 2.2 %shard_map.37 = bf16[32,72,128]{2,1,0:T(8,128)(2,1)} custom-call(f32[2,2,16,4096]{3,2,1,0:T(8,128)} %spectra_ref.1, s32[16,64]{1,0:T(8,128)} %bitcast.4), custom_call_target="tpu_custom_call" | custom-call | tf_op jit(solution)/shard_map/pallas_call | solution.py:44
  2.2 8.4 %all-to-all-start = ((bf16[32,72,128]{2,1,0:T(8,128)(2,1)}), bf16[32,72,128]{2,1,0:T(8,128)(2,1)S(1)}, u32[]{:S(2)}, u32[]{:S(2)}) async-start(bf16[32,72,128]{2,1,0:T(8,128)(2,1)} %shard_map.37), calls=%async_computation | async-start | bytes 1179648 | tf_op jit(solution)/shard_map/all_to_all | solution.py:170
  10.7 1.1 %fusion.4 = (f32[1,128,512]{2,1,0:T(8,128)S(1)}, f32[1,128,512]{2,1,0:T(8,128)S(1)}) fusion(s32[512]{0:T(512)S(1)} %iota_add_fusion, s32[128]{0:T(128)S(1)} %iota_add_fusion.1), kind=kLoop, calls=%fused_computation.13 | loop fusion | flops 983040 | bytes 526848 | tf_op jit(solution)/shard_map/cos | solution.py:159
  11.8 0.0 copy-start
  11.8 11.3 %all-to-all-done.x_ref = bf16[32,72,128]{2,1,0:T(8,128)(2,1)S(1)} async-done(((bf16[32,72,128]{2,1,0:T(8,128)(2,1)}), bf16[32,72,128]{2,1,0:T(8,128)(2,1)S(1)}, u32[]{:S(2)}, u32[]{:S(2)}) %all-to-all-start) | async-done | bytes 589856 | tf_op jit(solution)/shard_map/all_to_all | solution.py:170
  23.2 0.0 copy-done
  23.2 9.9 %shard_map.38 = bf16[256,512]{1,0:T(8,128)(2,1)} custom-call(s32[4]{0:T(128)S(1)} %copy-done, bf16[32,72,128]{2,1,0:T(8,128)(2,1)S(1)} %all-to-all-done.x_ref, bf16[256,512]{1,0:T(8,128)(2,1)S(1)} %bitcast.3), custom_call_target="tpu_custom_call" | custom-call | tf_op jit(solution)/shard_map/pallas_call | solution.py:138
  33.0 3.9 %all-to-all-start.1 = ((bf16[32,8,512]{2,1,0:T(8,128)(2,1)}), bf16[32,8,512]{2,1,0:T(8,128)(2,1)S(1)}, u32[]{:S(2)}, u32[]{:S(2)}) async-start(bf16[32,8,512]{2,1,0:T(8,128)(2,1)} %bitcast.2), calls=%async_computation.1 | async-start | bytes 524288 | tf_op jit(solution)/shard_map/all_to_all | solution.py:174
  36.9 0.3 convert_reduce_fusion
  37.2 8.6 %all-to-all-done.1 = bf16[32,8,512]{2,1,0:T(8,128)(2,1)S(1)} async-done(((bf16[32,8,512]{2,1,0:T(8,128)(2,1)}), bf16[32,8,512]{2,1,0:T(8,128)(2,1)S(1)}, u32[]{:S(2)}, u32[]{:S(2)}) %all-to-all-start.1) | async-done | bytes 262176 | tf_op jit(solution)/shard_map/all_to_all | solution.py:174
  45.8 2.8 %collective-permute-start.2 = (f32[8,512]{1,0:T(8,128)S(1)}, f32[8,512]{1,0:T(8,128)S(1)}, u32[]{:S(2)}, u32[]{:S(2)}) collective-permute-start(f32[8,512]{1,0:T(8,128)S(1)} %convert_reduce_fusion.1), channel_id=1, source_target_pairs={{0,3},{1,0},{2,1},{3,2},{4,7},{5,4},{6,5},{7,6},{8,11},{9,8},{10,9... | collective-permute-start | bytes 49160 | tf_op jit(solution)/shard_map/ppermute | solution.py:183
  48.7 0.8 %collective-permute-start.1 = (f32[8,512]{1,0:T(8,128)S(1)}, f32[8,512]{1,0:T(8,128)S(1)}, u32[]{:S(2)}, u32[]{:S(2)}) collective-permute-start(f32[8,512]{1,0:T(8,128)S(1)} %convert_reduce_fusion.1), channel_id=1, source_target_pairs={{0,2},{1,3},{2,0},{3,1},{4,6},{5,7},{6,4},{7,5},{8,10},{9,11},{10,... | collective-permute-start | bytes 49160 | tf_op jit(solution)/shard_map/ppermute | solution.py:183
  49.5 0.9 %collective-permute-start = (f32[8,512]{1,0:T(8,128)S(1)}, f32[8,512]{1,0:T(8,128)S(1)}, u32[]{:S(2)}, u32[]{:S(2)}) collective-permute-start(f32[8,512]{1,0:T(8,128)S(1)} %convert_reduce_fusion.1), channel_id=1, source_target_pairs={{0,1},{1,2},{2,3},{3,0},{4,5},{5,6},{6,7},{7,4},{8,9},{9,10},{10,1... | collective-permute-start | bytes 49160 | tf_op jit(solution)/shard_map/ppermute | solution.py:183
  50.4 0.0 collective-permute-done.2
  50.4 3.5 %collective-permute-done.1 = f32[8,512]{1,0:T(8,128)S(1)} collective-permute-done((f32[8,512]{1,0:T(8,128)S(1)}, f32[8,512]{1,0:T(8,128)S(1)}, u32[]{:S(2)}, u32[]{:S(2)}) %collective-permute-start.1) | collective-permute-done | bytes 16416 | tf_op jit(solution)/shard_map/ppermute | solution.py:183
  53.9 0.5 collective-permute-done
  54.4 0.7 %add_divide_fusion = f32[8,512]{1,0:T(8,128)} fusion(f32[8,512]{1,0:T(8,128)S(1)} %collective-permute-done.2, f32[8,512]{1,0:T(8,128)S(1)} %collective-permute-done.1, f32[8,512]{1,0:T(8,128)S(1)} %convert_reduce_fusion.1, f32[8,512]{1,0:T(8,128)S(1)} %collective-permute-done, f32[8]{0:T(128)S(1)} %multiply_sqrt_fusion), kind=kLoop, calls=%fused_computation.15 | loop fusion | flops 16384 | bytes 81952 | tf_op jit(solution)/shard_map/div | solution.py:186
  (7 shorter events, 0.1 us)
Async XLA Ops:
  2.2 21.0 %all-to-all-start = ((bf16[32,72,128]{2,1,0:T(8,128)(2,1)}), bf16[32,72,128]{2,1,0:T(8,128)(2,1)S(1)}, u32[]{:S(2)}, u32[]{:S(2)}) async-start(bf16[32,72,128]{2,1,0:T(8,128)(2,1)} %shard_map.37), calls=%async_computation | async-start | bytes 1179648 | tf_op jit(solution)/shard_map/all_to_all | solution.py:170
  11.8 11.3 %copy-start = (s32[4]{0:T(128)S(1)}, s32[4]{0:T(128)}, u32[]{:S(2)}) copy-start(s32[4]{0:T(128)} %plan_ref.1) | copy-start | bytes 52
  33.0 12.8 %all-to-all-start.1 = ((bf16[32,8,512]{2,1,0:T(8,128)(2,1)}), bf16[32,8,512]{2,1,0:T(8,128)(2,1)S(1)}, u32[]{:S(2)}, u32[]{:S(2)}) async-start(bf16[32,8,512]{2,1,0:T(8,128)(2,1)} %bitcast.2), calls=%async_computation.1 | async-start | bytes 524288 | tf_op jit(solution)/shard_map/all_to_all | solution.py:174
  45.8 4.5 %collective-permute-start.2 = (f32[8,512]{1,0:T(8,128)S(1)}, f32[8,512]{1,0:T(8,128)S(1)}, u32[]{:S(2)}, u32[]{:S(2)}) collective-permute-start(f32[8,512]{1,0:T(8,128)S(1)} %convert_reduce_fusion.1), channel_id=1, source_target_pairs={{0,3},{1,0},{2,1},{3,2},{4,7},{5,4},{6,5},{7,6},{8,11},{9,8},{10,9... | collective-permute-start | bytes 49160 | tf_op jit(solution)/shard_map/ppermute | solution.py:183
  48.7 5.2 %collective-permute-start.1 = (f32[8,512]{1,0:T(8,128)S(1)}, f32[8,512]{1,0:T(8,128)S(1)}, u32[]{:S(2)}, u32[]{:S(2)}) collective-permute-start(f32[8,512]{1,0:T(8,128)S(1)} %convert_reduce_fusion.1), channel_id=1, source_target_pairs={{0,2},{1,3},{2,0},{3,1},{4,6},{5,7},{6,4},{7,5},{8,10},{9,11},{10,... | collective-permute-start | bytes 49160 | tf_op jit(solution)/shard_map/ppermute | solution.py:183
  49.5 4.9 %collective-permute-start = (f32[8,512]{1,0:T(8,128)S(1)}, f32[8,512]{1,0:T(8,128)S(1)}, u32[]{:S(2)}, u32[]{:S(2)}) collective-permute-start(f32[8,512]{1,0:T(8,128)S(1)} %convert_reduce_fusion.1), channel_id=1, source_target_pairs={{0,1},{1,2},{2,3},{3,0},{4,5},{5,6},{6,7},{7,4},{8,9},{9,10},{10,1... | collective-permute-start | bytes 49160 | tf_op jit(solution)/shard_map/ppermute | solution.py:183
